TPU v7x, 512 devices: a whole 4x4x16 slice. The times are simulated.
512 devices in a mesh: tm: 16 (over x, y), node: 32 (over z, core).
Axes of the slice: x: 4, y: 4, z: 16, core: 2. Of those that a mesh axis runs over, the one named last changes fastest.
Arguments:
- message: bfloat16 [131072, 512], P(('tm', 'node')), may hold values from -6 to 6
- dest_mem: bfloat16 [131072, 512], P(('tm', 'node')), may hold values from -6 to 6
- nbr_rows: bfloat16 [786432, 512], P(('tm', 'node')), may hold values from -6 to 6
- emb_grad: bfloat16 [131072, 512], P(('tm', 'node')), may hold values from -6 to 6
- event_time: int32 [131072], P(('tm', 'node')), may hold values from 1000 to 1999
- nbr_time: int32 [131072, 6], P(('tm', 'node')), may hold values from 0 to 999
- nbr_count: int32 [131072], P(('tm', 'node')), may hold values from 1 to 6
- source_id: int32 [131072], P(('tm', 'node')), may hold values from 0 to 1023
- dest_local: int32 [131072], P(('tm', 'node')), may hold values from 0 to 31
- read_owner: int32 [786432, 1], P(('tm', 'node')), may hold values from 0 to 15; in each aligned block of 1536 rows (0 to 1535, 1536 to 3071, ...) at most 192 rows name the same one
- read_row: int32 [786432], P(('tm', 'node')), may hold values from 0 to 31
- w_in: bfloat16 [512, 1536], P('node'), may hold values from -0.25 to 0.25
- w_hid: bfloat16 [512, 1536], P('node'), may hold values from -0.25 to 0.25
- w_query: bfloat16 [512, 512], P('node'), may hold values from -0.25 to 0.25
- w_keyval: bfloat16 [512, 1024], P('node'), may hold values from -0.25 to 0.25
- w_out: bfloat16 [512, 512], P('node'), may hold values from -0.25 to 0.25
Outputs:
- version_grad: float32 [16384, 512], P(('tm', 'node'))
- node_grad: float32 [16, 1024, 512], P('tm', 'node')
Inputs may be any that keep to these rules, and one draw needn't show every extreme that they name: `read_owner`: no owner group is named by more than 192 of the reads of one device.
All inputs are finite; a program needn't handle non-finite values.
Results may differ from a plain program's by a relative error of at most 0.015.
Values may be sent and summed in bfloat16 or wider, within the bound.
A program may use at most 64 MiB of HBM per device.

v0:
```python
import math

import jax
import jax.numpy as jnp
from jax import lax
from jax.sharding import PartitionSpec as P

HEADS = 2
NODE_DEV = 32
VER_DEV = 32


def embed_events(message, dest_mem, key_in, slot_mask, weights):
    w_in, w_hid, w_query, w_keyval, w_out = weights
    features = message.shape[1]
    events = message.shape[0]
    neighbours = key_in.shape[1]
    head_size = features // HEADS
    gate_in = jnp.dot(message, w_in, preferred_element_type=jnp.float32)
    gate_hid = jnp.dot(dest_mem, w_hid, preferred_element_type=jnp.float32)
    reset_gate = jax.nn.sigmoid(gate_in[:, :features] + gate_hid[:, :features])
    update_gate = jax.nn.sigmoid(
        gate_in[:, features : 2 * features] + gate_hid[:, features : 2 * features]
    )
    candidate = jnp.tanh(gate_in[:, 2 * features :] + reset_gate * gate_hid[:, 2 * features :])
    memory = ((1.0 - update_gate) * candidate + update_gate * dest_mem.astype(jnp.float32)).astype(
        jnp.bfloat16
    )
    queries = jnp.dot(memory, w_query, preferred_element_type=jnp.float32).astype(jnp.bfloat16)
    queries = queries.reshape(events, HEADS, head_size)
    keyval = jnp.dot(
        key_in.reshape(events * neighbours, features), w_keyval, preferred_element_type=jnp.float32
    )
    keyval = keyval.astype(jnp.bfloat16).reshape(events, neighbours, 2, HEADS, head_size)
    score_scale = 1.0 / math.sqrt(head_size)
    scores = (
        jnp.einsum(
            "eah,ejah->eaj", queries.astype(jnp.float32), keyval[:, :, 0].astype(jnp.float32)
        )
        * score_scale
    )
    weight_raw = jnp.exp(scores) * slot_mask[:, None, :]
    attn_weights = (weight_raw / jnp.sum(weight_raw, axis=2, keepdims=True)).astype(jnp.bfloat16)
    attended = jnp.einsum(
        "eaj,ejah->eah", attn_weights.astype(jnp.float32), keyval[:, :, 1].astype(jnp.float32)
    )
    attended = attended.astype(jnp.bfloat16).reshape(events, features)
    return jnp.dot(attended, w_out, preferred_element_type=jnp.float32) + memory.astype(jnp.float32)


def backward(message, dest_mem, nbr_rows, emb_grad, event_time, nbr_time, nbr_count, weights):
    events = message.shape[0]
    features = message.shape[1]
    neighbours = nbr_time.shape[1]
    frequency = jnp.exp(
        jnp.arange(features, dtype=jnp.float32) * (-9.0 * math.log(10.0) / features)
    )
    time_gap = (event_time[:, None] - nbr_time).astype(jnp.float32)
    time_code = jnp.cos(time_gap[:, :, None] * frequency[None, None, :])
    key_in = (
        nbr_rows.reshape(events, neighbours, features).astype(jnp.float32) + time_code
    ).astype(jnp.bfloat16)
    slot_mask = (jnp.arange(neighbours, dtype=jnp.int32)[None, :] < nbr_count[:, None]).astype(
        jnp.float32
    )

    def local_embed(msg_part, dest_part, key_part):
        return embed_events(msg_part, dest_part, key_part, slot_mask, weights)

    _, pullback = jax.vjp(local_embed, message, dest_mem, key_in)
    grad_message, grad_dest, grad_key = pullback(emb_grad.astype(jnp.float32))
    return (grad_message, grad_dest, grad_key.reshape(events * neighbours, features))


def body(
    message,
    dest_mem,
    nbr_rows,
    emb_grad,
    event_time,
    nbr_time,
    nbr_count,
    source_id,
    dest_local,
    read_owner,
    read_row,
    w_in,
    w_hid,
    w_query,
    w_keyval,
    w_out,
):
    weights = (
        lax.all_gather(w_in, "node", axis=0, tiled=True),
        lax.all_gather(w_hid, "node", axis=0, tiled=True),
        lax.all_gather(w_query, "node", axis=0, tiled=True),
        lax.all_gather(w_keyval, "node", axis=0, tiled=True),
        lax.all_gather(w_out, "node", axis=0, tiled=True),
    )
    grad_message, grad_dest, grad_read = backward(
        message, dest_mem, nbr_rows, emb_grad, event_time, nbr_time, nbr_count, weights
    )
    read_total = nbr_rows.shape[0]
    features = nbr_rows.shape[1]
    groups = lax.axis_size("tm")
    capacity = 2 * read_total // groups
    owner_group = read_owner[:, 0]
    owner_table = (owner_group[:, None] == jnp.arange(groups, dtype=jnp.int32)[None, :]).astype(
        jnp.int32
    )
    slot_rank = jnp.sum((jnp.cumsum(owner_table, axis=0) - owner_table) * owner_table, axis=1)
    send_slot = owner_group * capacity + slot_rank
    send_rows = jnp.zeros((groups * capacity, features), jnp.bfloat16).at[send_slot].set(grad_read)
    send_index = jnp.full((groups * capacity,), VER_DEV, jnp.int32).at[send_slot].set(read_row)
    got_rows, got_index = (
        lax.all_to_all(
            send_rows.reshape(groups, capacity, features),
            "tm",
            split_axis=0,
            concat_axis=0,
            tiled=True,
        ),
        lax.all_to_all(
            send_index.reshape(groups, capacity), "tm", split_axis=0, concat_axis=0, tiled=True
        ),
    )
    one_hot = (
        jnp.arange(VER_DEV, dtype=jnp.int32)[:, None] == got_index.reshape(1, groups * capacity)
    ).astype(jnp.bfloat16)
    version_grad = jnp.dot(
        one_hot, got_rows.reshape(groups * capacity, features), preferred_element_type=jnp.float32
    )
    dest_ids = lax.axis_index("node") * NODE_DEV + dest_local
    node_ids = jnp.concatenate([source_id, dest_ids])
    both_grads = jnp.concatenate([grad_message, grad_dest])
    wanted = jnp.arange(NODE_DEV * lax.axis_size("node"), dtype=jnp.int32)
    one_hot = (wanted[:, None] == node_ids[None, :]).astype(jnp.bfloat16)
    node_grad = lax.psum_scatter(
        jnp.dot(one_hot, both_grads, preferred_element_type=jnp.float32),
        "node",
        scatter_dimension=0,
        tiled=True,
    )
    return (version_grad, node_grad[None])


def solution(mesh):
    in_specs = (
        P(("tm", "node"), None),
        P(("tm", "node"), None),
        P(("tm", "node"), None),
        P(("tm", "node"), None),
        P(("tm", "node")),
        P(("tm", "node"), None),
        P(("tm", "node")),
        P(("tm", "node")),
        P(("tm", "node")),
        P(("tm", "node"), None),
        P(("tm", "node")),
        P("node", None),
        P("node", None),
        P("node", None),
        P("node", None),
        P("node", None),
    )
    out_specs = (P(("tm", "node"), None), P("tm", "node", None))
    return jax.shard_map(body, mesh=mesh, in_specs=in_specs, out_specs=out_specs, check_vma=False)
```

profile of v0, /device:TPU:6, one launch (start us, length us, event | category | flops | bytes accessed | tf_op | source)
XLA Modules:
  0.0 372.1 jit_solution(16934541902874893013)
XLA Ops:
  9.4 4.5 %reduce-window.6 = s32[16,12,128]{2,1,0:T(8,128)S(1)} reduce-window(s32[16,12,128]{2,1,0:T(8,128)S(1)} %fusion.55, s32[]{:T(128)} %constant.12.clone.1), window={size=1x1x128 pad=0_0x0_0x127_0}, to_apply=%region_0.0 | reduce-window | flops 3121152 | bytes 196612 | tf_op jit(solution)/shard_map/reduce-window
  15.5 6.4 %scatter_custom_fusion = s32[3072]{0:T(1024)S(1)} fusion(s32[1536]{0:T(1024)S(1)} %fusion.60, s32[1536]{0:T(1024)} %param.26, s32[]{:T(128)} %constant.10.clone.1), kind=kCustom, calls=%fused_computation.104 | custom fusion | bytes 12800 | tf_op jit(solution)/shard_map/scatter | solution.py:114
  22.5 9.2 %all-to-all-start = ((s32[16,1,192]{2,1,0:T(1,128)}), s32[16,1,192]{2,1,0:T(1,128)S(1)}, u32[]{:S(2)}, u32[]{:S(2)}) async-start(s32[16,1,192]{2,1,0:T(1,128)} %all_to_all.9), calls=%async_computation | async-start | bytes 32768 | tf_op jit(solution)/shard_map/all_to_all | solution.py:123
  32.5 36.3 %all_gather.15 = bf16[512,512]{1,0:T(8,128)(2,1)S(1)} all-gather(bf16[16,512]{1,0:T(8,128)(2,1)} %param.31), channel_id=1, replica_groups=mesh['tm'=16,'node'=32] {'node'}, dimensions={0}, use_global_device_ids=true | all-gather | bytes 540672 | tf_op jit(solution)/shard_map/all_gather | solution.py:98
  72.2 31.2 %all_gather.18 = bf16[512,512]{1,0:T(8,128)(2,1)} all-gather(bf16[16,512]{1,0:T(8,128)(2,1)S(1)} %copy-done.21), channel_id=1, replica_groups=mesh['tm'=16,'node'=32] {'node'}, dimensions={0}, use_global_device_ids=true | all-gather | bytes 540672 | tf_op jit(solution)/shard_map/all_gather | solution.py:96
  103.4 15.0 %convolution_convert_fusion = bf16[1536,1024]{1,0:T(8,128)(2,1)} fusion(bf16[512,1024]{1,0:T(8,128)(2,1)} %all-gather.8.cloned.1.call-done, bf16[1536,512]{1,0:T(8,128)(2,1)S(1)} %copy-done.29, f32[512]{0:T(512)S(1)} %multiply_exponential_fusion, f32[1536]{0:T(1024)S(1)} %mul.132), kind=kOutput, calls=%fused_computation.2 | convolution fusion | flops 1615331328 | bytes 5775360 | tf_op jit(solution)/shard_map/jvp()/dot_general | solution.py:31
  118.4 4.8 %reshape.93 = bf16[256,6,2,2,256]{4,3,2,1,0:T(2,128)(2,1)S(1)} reshape(bf16[1536,1024]{1,0:T(8,128)(2,1)} %convolution_convert_fusion) | data formatting | bytes 6291456 | tf_op jit(solution)/shard_map/jvp()/reshape | solution.py:34
  123.2 3.2 slice_bitcast_fusion
  127.0 2.4 copy.24
  129.5 26.5 %all-gather.4.cloned.1.call-done = bf16[512,1536]{1,0:T(8,128)(2,1)} async-done(((bf16[16,1536]{1,0:T(8,128)(2,1)}), bf16[512,1536]{1,0:T(8,128)(2,1)}) %all-gather.4.cloned.1.call-update) | async-done | bytes 1572880 | tf_op jit(solution)/shard_map/all_gather | solution.py:94
  156.0 3.1 fusion.69
  159.1 67.3 %all-gather.6.cloned.1.call-done = bf16[512,1536]{1,0:T(8,128)(2,1)} async-done(((bf16[16,1536]{1,0:T(8,128)(2,1)}), bf16[512,1536]{1,0:T(8,128)(2,1)}) %all-gather.6.cloned.1.call-update) | async-done | bytes 1572880 | tf_op jit(solution)/shard_map/all_gather | solution.py:95
  226.5 2.1 fusion.70
  230.7 2.7 reshape.121
  233.4 1.7 reshape.92
  235.1 3.0 fusion.2
  238.1 2.6 copy.21
  242.4 1.9 fusion.38
  244.3 4.3 %copy.25 = bf16[256,2,6,1]{2,3,1,0:T(2,128)(2,1)S(1)} copy(f32[256,2,6,1]{1,2,0,3:T(8,128)} %bitcast.81) | data formatting | bytes 18432 | tf_op jit(solution)/shard_map/transpose(jvp())/mul | solution.py:37
  248.6 2.3 fusion
  252.1 1.1 copy-done.15
  255.3 2.1 fusion.6
  258.7 2.1 fusion.10
  260.8 2.2 fusion.9
  263.1 4.0 %pad_add_fusion = bf16[256,6,2,2,256]{4,3,2,1,0:T(2,128)(2,1)S(1)} fusion(bf16[256,6,1,2,256]{4,3,2,1,0:T(2,128)(2,1)S(1)} %fusion.10, bf16[256,6,1,2,256]{4,3,2,1,0:T(2,128)(2,1)S(1)} %fusion.9), kind=kLoop, calls=%fused_computation.3 | loop fusion | flops 1572864 | bytes 6291456 | tf_op jit(solution)/shard_map/transpose(jvp())/add_any | solution.py:38
  267.1 3.9 %reshape.94 = bf16[1536,1024]{1,0:T(8,128)(2,1)} reshape(bf16[256,6,2,2,256]{4,3,2,1,0:T(2,128)(2,1)S(1)} %pad_add_fusion) | data formatting | bytes 6291456 | tf_op jit(solution)/shard_map/transpose(jvp())/reshape | solution.py:34
  271.0 4.0 %convolution_convert_fusion.1 = bf16[1536,512]{1,0:T(8,128)(2,1)S(1)} fusion(bf16[1536,1024]{1,0:T(8,128)(2,1)} %reshape.94, bf16[512,1024]{1,0:T(8,128)(2,1)} %all-gather.8.cloned.1.call-done), kind=kOutput, calls=%fused_computation.7 | convolution fusion | flops 1611399168 | bytes 5767168 | tf_op jit(solution)/shard_map/transpose(jvp())/dot_general | solution.py:31
  275.1 9.6 %scatter_custom_fusion.1 = bf16[3072,512]{1,0:T(8,128)(2,1)} fusion(s32[1536]{0:T(1024)} %copy-done.23, bf16[1536,512]{1,0:T(8,128)(2,1)S(1)} %convolution_convert_fusion.1, bf16[]{:T(256)} %constant.14.clone.1), kind=kCustom, calls=%fused_computation.30 | custom fusion | bytes 3146240 | tf_op jit(solution)/shard_map/scatter | solution.py:113
  284.6 7.3 %all-to-all-start.1 = ((bf16[16,192,512]{2,1,0:T(8,128)(2,1)}), bf16[16,192,512]{2,1,0:T(8,128)(2,1)S(1)}, u32[]{:S(2)}, u32[]{:S(2)}) async-start(bf16[16,192,512]{2,1,0:T(8,128)(2,1)} %bitcast.9), calls=%async_computation.1 | async-start | bytes 6291456 | tf_op jit(solution)/shard_map/all_to_all | solution.py:116
  292.0 44.2 %all-to-all-done.1 = bf16[16,192,512]{2,1,0:T(8,128)(2,1)S(1)} async-done(((bf16[16,192,512]{2,1,0:T(8,128)(2,1)}), bf16[16,192,512]{2,1,0:T(8,128)(2,1)S(1)}, u32[]{:S(2)}, u32[]{:S(2)}) %all-to-all-start.1) | async-done | bytes 3145760 | tf_op jit(solution)/shard_map/all_to_all | solution.py:116
  336.2 1.2 fusion.51
  337.4 28.2 %reduce-scatter.2.cloned.1.call-done = f32[32,512]{1,0:T(8,128)} async-done(((f32[1024,512]{1,0:T(8,128)}), f32[32,512]{1,0:T(8,128)}) %reduce-scatter.2.cloned.1.call-update) | async-done | bytes 65552 | tf_op jit(solution)/shard_map/reduce_scatter | solution.py:138
  (104 shorter events, 17.6 us)
Async XLA Ops:
  7.2 148.8 %copy-start = (bf16[256,512]{1,0:T(8,128)(2,1)S(1)}, bf16[256,512]{1,0:T(8,128)(2,1)}, u32[]{:S(2)}) copy-start(bf16[256,512]{1,0:T(8,128)(2,1)} %param.16) | copy-start | bytes 786436
  7.2 61.6 %copy-start.18 = (bf16[256,512]{1,0:T(8,128)(2,1)S(1)}, bf16[256,512]{1,0:T(8,128)(2,1)}, u32[]{:S(2)}) copy-start(bf16[256,512]{1,0:T(8,128)(2,1)} %param.19) | copy-start | bytes 786436
  7.2 96.2 %all-gather.8.cloned.1.call-start = ((), (), s32[]{:S(2)}) async-start(), calls=%async_computation.5 | async-start | bytes 1081344 | tf_op jit(solution)/shard_map/all_gather | solution.py:97
  7.9 148.1 %all-gather.4.cloned.1.call-start = ((), (), s32[]{:S(2)}) async-start(), calls=%async_computation.3 | async-start | bytes 1622016 | tf_op jit(solution)/shard_map/all_gather | solution.py:94
  14.7 55.5 %copy-start.22 = (s32[256,6]{0,1:T(8,128)S(1)}, s32[256,6]{0,1:T(8,128)}, u32[]{:S(2)}) copy-start(s32[256,6]{0,1:T(8,128)} %param.21) | copy-start | bytes 18436
  14.7 55.5 %copy-start.26 = (s32[256]{0:T(256)S(1)}, s32[256]{0:T(256)}, u32[]{:S(2)}) copy-start(s32[256]{0:T(256)} %param.20) | copy-start | bytes 3076
  15.5 17.1 %copy-start.23 = (s32[1536]{0:T(1024)}, s32[1536]{0:T(1024)S(1)}, u32[]{:S(2)}) copy-start(s32[1536]{0:T(1024)S(1)} %fusion.60) | copy-start | bytes 18436
  22.5 262.1 %all-to-all-start = ((s32[16,1,192]{2,1,0:T(1,128)}), s32[16,1,192]{2,1,0:T(1,128)S(1)}, u32[]{:S(2)}, u32[]{:S(2)}) async-start(s32[16,1,192]{2,1,0:T(1,128)} %all_to_all.9), calls=%async_computation | async-start | bytes 32768 | tf_op jit(solution)/shard_map/all_to_all | solution.py:123
  31.8 194.7 %all-gather.6.cloned.1.call-start = ((), (), s32[]{:S(2)}) async-start(), calls=%async_computation.4 | async-start | bytes 1622016 | tf_op jit(solution)/shard_map/all_gather | solution.py:95
  32.5 333.1 %reduce-scatter.2.cloned.1.call-start = ((), (), s32[]{:S(2)}) async-start(), calls=%async_computation.6 | async-start | bytes 2162688 | tf_op jit(solution)/shard_map/reduce_scatter | solution.py:138
  68.8 2.7 copy-start.27
  68.8 2.7 copy-start.28
  68.8 3.3 copy-start.25
  68.8 3.4 copy-start.21
  69.2 34.2 %copy-start.29 = (bf16[1536,512]{1,0:T(8,128)(2,1)S(1)}, bf16[1536,512]{1,0:T(8,128)(2,1)}, u32[]{:S(2)}) copy-start(bf16[1536,512]{1,0:T(8,128)(2,1)} %param.18) | copy-start | bytes 4718596
  123.2 3.2 copy-start.20
  129.5 97.0 %copy-start.11 = (bf16[256,512]{1,0:T(8,128)(2,1)S(1)}, bf16[256,512]{1,0:T(8,128)(2,1)}, u32[]{:S(2)}) copy-start(bf16[256,512]{1,0:T(8,128)(2,1)} %param.17) | copy-start | bytes 786436
  226.5 2.1 copy-start.1
  228.6 1.1 copy-start.12
  229.0 6.1 %copy-start.6 = (f32[256,512]{1,0:T(8,128)}, f32[256,512]{1,0:T(8,128)S(1)}, u32[]{:S(2)}) copy-start(f32[256,512]{1,0:T(8,128)S(1)} %get-tuple-element.7) | copy-start | bytes 1572868
  229.0 6.1 %copy-start.8 = (f32[256,512]{1,0:T(8,128)}, f32[256,512]{1,0:T(8,128)S(1)}, u32[]{:S(2)}) copy-start(f32[256,512]{1,0:T(8,128)S(1)} %get-tuple-element.6) | copy-start | bytes 1572868
  248.6 2.6 copy-start.2
  248.6 2.6 copy-start.7
  248.6 2.6 copy-start.9
  248.6 2.6 copy-start.13
  248.6 2.6 copy-start.19
  251.8 1.4 copy-start.15
  253.3 1.4 copy-start.16
  257.4 1.3 copy-start.3
  258.7 2.1 copy-start.10
  258.7 2.1 copy-start.14
  284.6 51.5 %all-to-all-start.1 = ((bf16[16,192,512]{2,1,0:T(8,128)(2,1)}), bf16[16,192,512]{2,1,0:T(8,128)(2,1)S(1)}, u32[]{:S(2)}, u32[]{:S(2)}) async-start(bf16[16,192,512]{2,1,0:T(8,128)(2,1)} %bitcast.9), calls=%async_computation.1 | async-start | bytes 6291456 | tf_op jit(solution)/shard_map/all_to_all | solution.py:116
  (4 other events, 3.7 us)
Sparse Core Ops, SparseCore 0:
  10.1 75.2 all-gather.7
  87.6 68.3 all-gather.3
  158.1 68.2 all-gather.5
  257.6 107.9 reduce-scatter.1
where the time goes:
time: 373 us; the launch traced here: 372 us
  waiting for transfers between devices  168 us (45%)
  blocking collectives  67.4 us (18%)
  local copies, waits for them, and re-layouts  48.5 us (13%)
  matrix products  36.6 us (10%)
  other arithmetic  20.3 us (5%)
  starting transfers between devices  16.6 us (4%)
  between operations  14.3 us (4%)
    all_gather x1, waiting for transfers between devices, body(): lax.all_gather(w_hid, 'node', axis=0, tiled=True)  67.3 us
    all_to_all x1, waiting for transfers between devices, body(): lax.all_to_all(send_rows.reshape(groups, capacity, features), 'tm', split...  44.2 us
    all_gather x1, blocking collectives, body(): lax.all_gather(w_out, 'node', axis=0, tiled=True)  36.3 us
    all_gather x1, blocking collectives, body(): lax.all_gather(w_query, 'node', axis=0, tiled=True)  31.2 us
    reduce_scatter x1, waiting for transfers between devices, body(): lax.psum_scatter(jnp.dot(one_hot, both_grads, preferred_element_type=jnp....  28.2 us
    all_gather x1, waiting for transfers between devices, body(): lax.all_gather(w_in, 'node', axis=0, tiled=True)  26.5 us
    dot_general x2, matrix products, embed_events(): jnp.dot(key_in.reshape(events * neighbours, features), w_keyval, preferre...  19 us
    scatter x1, local copies, waits for them, and re-layouts, body(): jnp.zeros((groups * capacity, features), jnp.bfloat16).at[send_slot]  9.56 us
  transfers between devices with their start and end apart: 6, of which 4 were waited for; matrix products, arithmetic and copies ran while one was open for 27% of the time, Pallas kernels for 0%

commit v1 on v0

v1 whole, which is shorter than its diff:
```python
import functools
import math

import jax
import jax.numpy as jnp
from jax import lax
from jax.experimental import pallas as pl
from jax.experimental.pallas import tpu as pltpu
from jax.sharding import PartitionSpec as P

D = 512
HEAD = 256
SLOTS = 6
EV = 256
READS = EV * SLOTS
OWN = 32
CA = 512
CB = 768
F32 = jnp.float32
BF16 = jnp.bfloat16
MESH = pl.DeviceIdType.MESH
FAR = ((5, 6, 7, 8), (9, 10, 11, 12), (1, 2, 3, 4), (13, 14, 15, 0))


def nn(a, b):
    return lax.dot_general(a, b, (((1,), (0,)), ((), ())), preferred_element_type=F32)


def nt(a, b):
    return lax.dot_general(a, b, (((1,), (1,)), ((), ())), preferred_element_type=F32)


def sigmoid(v):
    return 0.5 * jnp.tanh(0.5 * v) + 0.5


def cos_wide(angle):
    half = 0.5 * angle
    turns = jnp.floor(half * (1.0 / math.pi) + 0.5)
    s = (half - turns * 3.140625) - turns * (math.pi - 3.140625)
    q = s * s
    p = q * (-1.0 / 39916800.0) + (1.0 / 362880.0)
    p = p * q + (-1.0 / 5040.0)
    p = p * q + (1.0 / 120.0)
    p = p * q + (-1.0 / 6.0)
    p = p * q + 1.0
    sine = p * s
    return 1.0 - 2.0 * (sine * sine)


def cos_small(angle):
    q = angle * angle
    return 1.0 + q * (q * (1.0 / 24.0) - 0.5)


def kernel(
    msg, dst, nbr, emb, ev_time, nb_time, nb_count, src_id, dst_loc, owner, vrow,
    w_in, w_hid, w_q, w_kv, w_out,
    ver_out, node_out,
    wa, wb, rbuf, keys, gkb, qk, gv, ctx, gates, gmem, gin, gcand, gmsg, tcol, tpack, gwp, scp, wtp,
    vpart, vbuf, npart, nsib, nsend, nrecv, dpart,
    loc_sem, s1_send, s1_recv, r1_send, r2_send, piece_sem, sib_send, sib_recv,
    v_send, v_recv, nd_send, nd_recv, ring_send, ring_recv,
):
    tm = lax.axis_index("tm")
    node = lax.axis_index("node")
    x, y = tm // 4, tm % 4
    z, c = node // 2, node % 2
    other = 1 - c
    sibling = (tm, z * 2 + other)
    zq, zy = z // 4, z % 4

    def pick(p, q):
        return jnp.where(c == 0, p, q)

    a, b = pick(x, y), pick(y, x)

    def tm_of(aa, bb):
        return pick(aa * 4 + bb, bb * 4 + aa)

    a_left, a_right, a_far = (a + 3) % 4, (a + 1) % 4, (a + 2) % 4
    b_left, b_right, b_far = (b + 3) % 4, (b + 1) % 4, (b + 2) % 4
    dev_a_left, dev_a_right = (tm_of(a_left, b), node), (tm_of(a_right, b), node)
    dev_b_left, dev_b_right = (tm_of(a, b_left), node), (tm_of(a, b_right), node)

    bufs = ((wa, CA), (wb, CB))

    def share(ph, q):
        buf, width = bufs[ph]
        return buf.at[q, y, c, :, pl.ds(pl.multiple_of(x * width, 128), width)]

    blocks = (((w_kv, 0), (w_in, 0)), ((w_kv, CA), (w_in, CB)), ((w_out, 0), (w_hid, 0)), ((w_q, 0), (w_hid, CB)))
    for k, pair in enumerate(blocks):
        @pl.when(jnp.logical_and(zy == y, x == k))
        def _(pair=pair):
            for ph, (ref, at) in enumerate(pair):
                pltpu.make_async_copy(
                    ref.at[:, pl.ds(at, bufs[ph][1])], share(ph, zq), loc_sem.at[ph]
                ).start()

    barrier = pltpu.get_barrier_semaphore()

    def greet(k, carry):
        pl.semaphore_signal(barrier, inc=1, device_id=(tm, (node + 2 * k) % 32), device_id_type=MESH)
        pl.semaphore_signal(barrier, inc=1, device_id=((tm + k) % 16, node), device_id_type=MESH)
        return carry

    lax.fori_loop(1, 16, greet, 0)
    pl.semaphore_signal(barrier, inc=1, device_id=sibling, device_id_type=MESH)

    pl.semaphore_wait(barrier, 31)

    @pl.when(zy == y)
    def _():
        for ph in range(2):
            def send(k, carry, ph=ph):
                pltpu.make_async_remote_copy(
                    src_ref=share(ph, zq), dst_ref=share(ph, zq),
                    send_sem=s1_send.at[ph], recv_sem=s1_recv.at[ph, zq],
                    device_id=(tm, ((z + k) % 16) * 2 + c), device_id_type=MESH,
                ).start()
                return carry
            pltpu.make_async_copy(share(ph, zq), share(ph, zq), loc_sem.at[ph]).wait()
            lax.fori_loop(1, 16, send, 0)

    def stage1_wait(ph):
        for q in range(4):
            @pl.when(4 * q + y != z)
            def _(q=q):
                pltpu.make_async_copy(share(ph, q), share(ph, q), s1_recv.at[ph, q]).wait()

    def piece(ph, aa, bb, part=None):
        buf, width = bufs[ph]
        xx, yy = pick(aa, bb), pick(bb, aa)
        rows = pl.ds(0, 4) if part is None else pl.ds(2 * part, 2)
        return buf.at[rows, yy, c, :, pl.ds(pl.multiple_of(xx * width, 128), width)]

    def send_piece(ph, aa, bb, device, send_sem, part=None, slot=0):
        ref = piece(ph, aa, bb, part)
        pltpu.make_async_remote_copy(
            src_ref=ref, dst_ref=ref, send_sem=send_sem.at[ph],
            recv_sem=piece_sem.at[ph, aa * 4 + bb, slot],
            device_id=device, device_id_type=MESH,
        ).start()

    def wait_piece(ph, aa, bb, part=None, slot=0):
        ref = piece(ph, aa, bb, part)
        pltpu.make_async_copy(ref, ref, piece_sem.at[ph, aa * 4 + bb, slot]).wait()

    def to_sibling(ph, aa, bb):
        ref = piece(ph, aa, bb)
        pltpu.make_async_remote_copy(
            src_ref=ref, dst_ref=ref, send_sem=sib_send.at[ph], recv_sem=sib_recv.at[ph],
            device_id=sibling, device_id_type=MESH,
        ).start()

    def second_ring(ph, aa):
        send_piece(ph, aa, b, dev_b_left, r2_send)
        send_piece(ph, aa, b, dev_b_right, r2_send)
        to_sibling(ph, aa, b)

    def step0(ph):
        stage1_wait(ph)
        send_piece(ph, a, b, dev_a_left, r1_send)
        send_piece(ph, a, b, dev_a_right, r1_send)
        second_ring(ph, a)

    def step1(ph):
        wait_piece(ph, a_left, b)
        send_piece(ph, a_left, b, dev_a_right, r1_send, 0, 0)
        second_ring(ph, a_left)
        wait_piece(ph, a_right, b)
        send_piece(ph, a_right, b, dev_a_left, r1_send, 1, 1)
        second_ring(ph, a_right)

    def step2(ph):
        wait_piece(ph, a_far, b, 0, 0)
        wait_piece(ph, a_far, b, 1, 1)
        second_ring(ph, a_far)

    def step3(ph):
        for aa in (a, a_left, a_right, a_far):
            wait_piece(ph, aa, b_left)
            send_piece(ph, aa, b_left, dev_b_right, r2_send, 0, 0)
            to_sibling(ph, aa, b_left)
            wait_piece(ph, aa, b_right)
            send_piece(ph, aa, b_right, dev_b_left, r2_send, 1, 1)
            to_sibling(ph, aa, b_right)

    def step4(ph):
        for aa in (a, a_left, a_right, a_far):
            wait_piece(ph, aa, b_far, 0, 0)
            wait_piece(ph, aa, b_far, 1, 1)
            to_sibling(ph, aa, b_far)

    def all_here(ph):
        ref = bufs[ph][0].at[:, :, other]
        pltpu.make_async_copy(ref, ref, sib_recv.at[ph]).wait()

    def widen(i, carry):
        at = pl.ds(pl.multiple_of(i * 64, 64), 64)
        for t in range(4):
            rbuf[t, at, :] = nbr[at, t * 128 : (t + 1) * 128].astype(F32)
        return carry

    lax.fori_loop(0, READS // 64, widen, 0)
    tpack[0:6, :] = (ev_time[...] - nb_time[...]).astype(F32)
    tpack[6:7, :] = nb_count[...].astype(F32)
    tpack[7:8, :] = jnp.zeros((1, EV), F32)
    tcol[...] = jnp.transpose(tpack[...])
    lanes = lax.broadcasted_iota(jnp.int32, (1, D), 1).astype(F32)
    freq = jnp.exp(lanes * (-9.0 * math.log(10.0) / D))

    def make_keys(i, carry):
        at = pl.ds(pl.multiple_of(i * 16, 16), 16)
        gaps = tcol[at, :]
        for j in range(SLOTS):
            gap = gaps[:, j : j + 1]
            for t, cosine in enumerate((cos_wide, cos_wide, cos_small, cos_small)):
                cut = slice(t * 128, (t + 1) * 128)
                rows = rbuf[t, pl.ds(i * (16 * SLOTS) + j, 16, stride=SLOTS), :]
                keys[j, at, cut] = rows + cosine(gap * freq[:, cut])
        return carry

    lax.fori_loop(0, EV // 16, make_keys, 0)

    step0(0)
    step0(1)
    step1(0)
    step2(0)
    step1(1)
    step2(1)
    step3(0)
    step4(0)
    step3(1)

    all_here(0)

    def wide(ref, start, width):
        return ref[:, :, :, :, pl.ds(start, width)].reshape(D, width)

    gatt = nt(emb[...], wide(wa, 1024, 512)).astype(BF16)
    for h in range(2):
        gv[h] = nt(gatt[:, h * HEAD : (h + 1) * HEAD], wide(wa, 512 + h * HEAD, HEAD))

    lane16 = lax.broadcasted_iota(jnp.int32, (16, 128), 1)

    def row_dots(vec, out):
        def block(i, carry):
            at = pl.ds(pl.multiple_of(i * 16, 16), 16)
            acc = jnp.zeros((16, 128), F32)
            v0, v1 = vec[0, at, :], vec[1, at, :]
            for j in range(SLOTS):
                key = keys[j, at, :]
                for h, v in enumerate((v0, v1)):
                    prod = key * v
                    part = (prod[:, 0:128] + prod[:, 128:256]) + (prod[:, 256:384] + prod[:, 384:512])
                    acc = jnp.where(lane16 == h * SLOTS + j, jnp.sum(part, axis=1, keepdims=True), acc)
            out[at, :] = acc
            return carry
        lax.fori_loop(0, EV // 16, block, 0)

    row_dots(gv, gwp)

    step4(1)
    all_here(1)

    def gate(k):
        return (nn(msg[...], wide(wb, k * D, D)), nn(dst[...], wide(wb, 1536 + k * D, D)))

    gi, gh = gate(0)
    reset = sigmoid(gi + gh)
    gates[0] = reset
    gi, gh = gate(2)
    gates[3] = gh
    gates[2] = jnp.tanh(gi + gates[0] * gh)
    gi, gh = gate(1)
    update = sigmoid(gi + gh)
    gates[1] = update
    memory = ((1.0 - update) * gates[2] + update * dst[...].astype(F32)).astype(BF16)
    quer = nn(memory, wide(wa, 1536, 512)).astype(BF16)
    for h in range(2):
        qk[h] = nt(quer[:, h * HEAD : (h + 1) * HEAD], wide(wa, h * HEAD, HEAD))

    row_dots(qk, scp)

    lane = lax.broadcasted_iota(jnp.int32, (EV, 128), 1)
    slot = jnp.where(lane >= SLOTS, lane - SLOTS, lane).astype(F32)
    head0, head1 = lane < SLOTS, jnp.logical_and(lane >= SLOTS, lane < 2 * SLOTS)
    live = jnp.logical_and(lane < 2 * SLOTS, slot < tcol[:, 6:7])
    raw = jnp.where(live, jnp.exp(scp[...] * (1.0 / 16.0)), 0.0)

    def per_head(v):
        s0 = jnp.sum(jnp.where(head0, v, 0.0), axis=1, keepdims=True)
        s1 = jnp.sum(jnp.where(head1, v, 0.0), axis=1, keepdims=True)
        return jnp.where(head0, s0, s1)

    weight = raw / per_head(raw)
    gw = gwp[...]
    wtp[...] = weight
    scp[...] = weight * (gw - per_head(weight * gw)) * (1.0 / 16.0)

    def spread(i, carry):
        at = pl.ds(pl.multiple_of(i * 16, 16), 16)
        sc, wt = scp[at, :], wtp[at, :]
        for lo in (0, 256):
            cut = slice(lo, lo + 256)
            q0, q1, g0, g1 = qk[0, at, cut], qk[1, at, cut], gv[0, at, cut], gv[1, at, cut]
            c0 = jnp.zeros((16, 256), F32)
            c1 = jnp.zeros((16, 256), F32)
            for j in range(SLOTS):
                s0, s1 = sc[:, j : j + 1], sc[:, SLOTS + j : SLOTS + j + 1]
                w0, w1 = wt[:, j : j + 1], wt[:, SLOTS + j : SLOTS + j + 1]
                key = keys[j, at, cut]
                c0 = c0 + s0 * key
                c1 = c1 + s1 * key
                for half in range(0, 256, 128):
                    hs = slice(half, half + 128)
                    rbuf[(lo + half) // 128, pl.ds(i * (16 * SLOTS) + j, 16, stride=SLOTS), :] = (
                        (s0 * q0[:, hs] + s1 * q1[:, hs]) + (w0 * g0[:, hs] + w1 * g1[:, hs])
                    )
            ctx[0, at, cut] = c0.astype(BF16)
            ctx[1, at, cut] = c1.astype(BF16)
        return carry

    lax.fori_loop(0, EV // 16, spread, 0)

    def narrow(i, carry):
        at = pl.ds(pl.multiple_of(i * 64, 64), 64)
        for t in range(4):
            gkb[at, t * 128 : (t + 1) * 128] = rbuf[t, at, :].astype(BF16)
        return carry

    lax.fori_loop(0, READS // 64, narrow, 0)

    vid = owner[...] * OWN + vrow[...]
    for m in range(2):
        hot = (lax.broadcasted_iota(jnp.int32, (256, READS), 0) + 256 * m == vid).astype(F32).astype(BF16)
        sums = nn(hot, gkb[...]).astype(BF16)
        vpart[pl.ds(8 * m, 8)] = sums.reshape(8, OWN, D)

    def send_versions(k, carry):
        to = (tm + k) % 16
        pltpu.make_async_remote_copy(
            src_ref=vpart.at[to], dst_ref=vbuf.at[k - 1],
            send_sem=v_send, recv_sem=v_recv,
            device_id=(to, node), device_id_type=MESH,
        ).start()
        return carry

    lax.fori_loop(1, 16, send_versions, 0)

    gq = [nn(ctx[h], wide(wa, h * HEAD, HEAD)).astype(BF16) for h in range(2)]
    gmem[...] = emb[...].astype(F32) + (
        nt(gq[0], wide(wa, 1536, HEAD)) + nt(gq[1], wide(wa, 1536 + HEAD, HEAD))
    )

    def gru(i, carry):
        at = pl.ds(pl.multiple_of(i * 16, 16), 16)
        gm = gmem[at, :]
        r, u, cand, hc = gates[0, at, :], gates[1, at, :], gates[2, at, :], gates[3, at, :]
        gu = gm * (dst[at, :].astype(F32) - cand)
        gc = gm * (1.0 - u) * (1.0 - cand * cand)
        gin[at, 0:512] = (gc * hc * (r * (1.0 - r))).astype(BF16)
        gin[at, 512:1024] = (gu * (u * (1.0 - u))).astype(BF16)
        gin[at, 1024:1536] = gc.astype(BF16)
        gcand[at, :] = (gc * r).astype(BF16)
        gmem[at, :] = gm * u
        return carry

    lax.fori_loop(0, EV // 16, gru, 0)

    gmsg[...] = nt(gin[...], wide(wb, 0, 1536)).astype(BF16)

    def part_copy(g):
        ref_from, ref_to = npart.at[g, other], nsib.at[g]
        return pltpu.make_async_remote_copy(
            src_ref=ref_from, dst_ref=ref_to, send_sem=nd_send.at[g], recv_sem=nd_recv.at[g],
            device_id=sibling, device_id_type=MESH,
        )

    for g, offsets in enumerate(FAR):
        base = ((z + offsets[0]) % 16) * 64
        wanted = (lax.broadcasted_iota(jnp.int32, (256, EV), 0) + base) & 1023
        hot = (wanted == src_id[...]).astype(F32).astype(BF16)
        sums = nn(hot, gmsg[...]).astype(BF16).reshape(4, 2, OWN, D)
        npart[g, 0] = sums[:, 0]
        npart[g, 1] = sums[:, 1]
        part_copy(g).start()

    def mine(rel):
        for g, offsets in enumerate(FAR):
            if rel in offsets:
                k = offsets.index(rel)
                return npart[g, c, k].astype(F32) + nsib[g, k].astype(F32)

    def hop(way, s):
        to = (z + 15) % 16 if way == 0 else (z + 1) % 16
        return pltpu.make_async_remote_copy(
            src_ref=nsend.at[way, s], dst_ref=nrecv.at[way, s],
            send_sem=ring_send.at[way, s], recv_sem=ring_recv.at[way, s],
            device_id=(tm, to * 2 + c), device_id_type=MESH,
        )

    part_copy(0).wait()
    nsend[0, 0] = mine(8).astype(BF16)
    hop(0, 0).start()
    nsend[1, 0] = mine(7).astype(BF16)
    hop(1, 0).start()

    gdst = (nt(gin[:, 0:1024], wide(wb, 1536, 1024)) + nt(gcand[...], wide(wb, 2560, 512))) + gmem[...]
    hot = (lax.broadcasted_iota(jnp.int32, (OWN, EV), 0) == dst_loc[...]).astype(F32).astype(BF16)
    dpart[...] = nn(hot, gdst.astype(BF16))

    for g in range(1, 4):
        part_copy(g).wait()

    for s in range(1, 8):
        hop(0, s - 1).wait_recv()
        nsend[0, s] = (mine(8 + s) + nrecv[0, s - 1].astype(F32)).astype(BF16)
        hop(0, s).start()
        if s < 7:
            hop(1, s - 1).wait_recv()
            nsend[1, s] = (mine(7 - s) + nrecv[1, s - 1].astype(F32)).astype(BF16)
            hop(1, s).start()
        if s == 4:
            pltpu.make_async_copy(vbuf, vbuf, v_recv).wait()
            total = vpart[tm].astype(F32)
            for k in range(15):
                total = total + vbuf[k].astype(F32)
            ver_out[...] = total
    hop(0, 7).wait_recv()
    hop(1, 6).wait_recv()
    node_out[...] = (mine(0) + dpart[...]) + (nrecv[0, 7].astype(F32) + nrecv[1, 6].astype(F32))

    for s in range(8):
        hop(0, s).wait_send()
        if s < 7:
            hop(1, s).wait_send()
    pltpu.make_async_copy(vbuf, vbuf, v_send).wait()
    for ph, (buf, width) in enumerate(bufs):
        ref = buf.at[:, :, c]
        pltpu.make_async_copy(ref, ref, sib_send.at[ph]).wait()
        ref = buf.at[:, 0:3, c, :, 0:width]
        pltpu.make_async_copy(ref, ref, r1_send.at[ph]).wait()
        ref = buf.at[:, 0:3, c]
        pltpu.make_async_copy(ref, ref, r2_send.at[ph]).wait()

    @pl.when(zy == y)
    def _():
        ref = wa.at[:, 0, c, :, 0:1920]
        pltpu.make_async_copy(ref, ref, s1_send.at[0]).wait()
        ref = wb.at[0, 0:3, :, :, 0:1920]
        pltpu.make_async_copy(ref, ref, s1_send.at[1]).wait()


def body(
    message, dest_mem, nbr_rows, emb_grad, event_time, nbr_time, nbr_count, source_id, dest_local,
    read_owner, read_row, w_in, w_hid, w_query, w_keyval, w_out,
):
    vmem = pl.BlockSpec(memory_space=pltpu.VMEM)
    hbm = pl.BlockSpec(memory_space=pl.ANY)
    dma = pltpu.SemaphoreType.DMA
    scratch = [
        pltpu.VMEM((4, 4, 2, 16, 2048), BF16),
        pltpu.VMEM((4, 4, 2, 16, 3072), BF16),
        pltpu.VMEM((4, READS, 128), F32),
        pltpu.VMEM((SLOTS, EV, D), F32),
        pltpu.VMEM((READS, D), BF16),
        pltpu.VMEM((2, EV, D), F32),
        pltpu.VMEM((2, EV, D), F32),
        pltpu.VMEM((2, EV, D), BF16),
        pltpu.VMEM((4, EV, D), F32),
        pltpu.VMEM((EV, D), F32),
        pltpu.VMEM((EV, 3 * D), BF16),
        pltpu.VMEM((EV, D), BF16),
        pltpu.VMEM((EV, D), BF16),
        pltpu.VMEM((EV, 8), F32),
        pltpu.VMEM((8, EV), F32),
        pltpu.VMEM((EV, 128), F32),
        pltpu.VMEM((EV, 128), F32),
        pltpu.VMEM((EV, 128), F32),
        pltpu.VMEM((16, OWN, D), BF16),
        pltpu.VMEM((15, OWN, D), BF16),
        pltpu.VMEM((4, 2, 4, OWN, D), BF16),
        pltpu.VMEM((4, 4, OWN, D), BF16),
        pltpu.VMEM((2, 8, OWN, D), BF16),
        pltpu.VMEM((2, 8, OWN, D), BF16),
        pltpu.VMEM((OWN, D), F32),
        dma((2,)),
        dma((2,)),
        dma((2, 4)),
        dma((2,)),
        dma((2,)),
        dma((2, 16, 2)),
        dma((2,)),
        dma((2,)),
        dma,
        dma,
        dma((4,)),
        dma((4,)),
        dma((2, 8)),
        dma((2, 8)),
    ]
    version_grad, node_grad = pl.pallas_call(
        kernel,
        out_shape=(jax.ShapeDtypeStruct((OWN, D), F32), jax.ShapeDtypeStruct((OWN, D), F32)),
        in_specs=[vmem] * 11 + [hbm] * 5,
        out_specs=(vmem, vmem),
        scratch_shapes=scratch,
        compiler_params=pltpu.CompilerParams(
            collective_id=0, has_side_effects=True, vmem_limit_bytes=56 * 1024 * 1024
        ),
        cost_estimate=pl.CostEstimate(
            flops=4_000_000_000, bytes_accessed=8_000_000, transcendentals=1_000_000
        ),
    )(
        message, dest_mem, nbr_rows, emb_grad,
        event_time.reshape(1, EV), nbr_time.T, nbr_count.reshape(1, EV),
        source_id.reshape(1, EV), dest_local.reshape(1, EV),
        read_owner.reshape(1, READS), read_row.reshape(1, READS),
        w_in, w_hid, w_query, w_keyval, w_out,
    )
    return version_grad, node_grad[None]


def solution(mesh):
    both = P(("tm", "node"))
    in_specs = (
        (P(("tm", "node"), None),) * 4
        + (both, P(("tm", "node"), None), both, both, both, P(("tm", "node"), None), both)
        + (P("node", None),) * 5
    )
    out_specs = (P(("tm", "node"), None), P("tm", "node", None))
    return jax.shard_map(body, mesh=mesh, in_specs=in_specs, out_specs=out_specs, check_vma=False)
```

time: 373 us -> 96.2 us (0.26)
  waiting for transfers between devices: 168 us -> 0 us
  Pallas kernels: 0 us -> 90.9 us
  blocking collectives: 67.4 us -> 0 us
  local copies, waits for them, and re-layouts: 48.5 us -> 4.24 us
  matrix products: 36.6 us -> 0 us
  other arithmetic: 20.3 us -> 0 us
  starting transfers between devices: 16.6 us -> 0 us
  between operations: 14.3 us -> 0.64 us
    all_gather x3 -> x0, waiting for transfers between devices: 93.9 us -> none  [the longest x1 67.3 us: body(): lax.all_gather(w_hid, 'node', axis=0, tiled=True)]
    pallas_call x0 -> x1, Pallas kernels: none -> 90.9 us  [body(): pl.pallas_call(kernel, out_shape=(jax.ShapeDtypeStruct((OWN, D), F32), ja...]
    all_gather x2 -> x0, blocking collectives: 67.4 us -> none  [the longest x1 36.3 us: body(): lax.all_gather(w_out, 'node', axis=0, tiled=True)]
    all_to_all x2 -> x0, waiting for transfers between devices: 44.2 us -> none  [the longest x1 44.2 us: body(): lax.all_to_all(send_rows.reshape(groups, capacity, features), 'tm', split...]
    dot_general x14 -> x0, matrix products: 36.6 us -> none  [the longest x2 19 us: embed_events(): jnp.dot(key_in.reshape(events * neighbours, features), w_keyval, preferre...]
    reduce_scatter x1 -> x0, waiting for transfers between devices: 28.2 us -> none  [body(): lax.psum_scatter(jnp.dot(one_hot, both_grads, preferred_element_type=jnp....]
    all_to_all x2 -> x0, starting transfers between devices: 16.5 us -> none  [the longest x1 9.21 us: body(): lax.all_to_all(send_index.reshape(groups, capacity), 'tm', split_axis=0,...]
    scatter x2 -> x0, local copies, waits for them, and re-layouts: 15.9 us -> none  [the longest x1 9.56 us: body(): jnp.zeros((groups * capacity, features), jnp.bfloat16).at[send_slot]]
  transfers between devices with their start and end apart: 6 -> 0, of which waited for: 4 -> 0; matrix products, arithmetic and copies ran while one was open for 27% -> 0% of each run, Pallas kernels for 0% -> 0%
where the time goes in v1:
time: 96.2 us; the launch traced here: 95.8 us
  Pallas kernels  90.9 us (94%)
  local copies, waits for them, and re-layouts  4.24 us (4%)
    pallas_call x1, Pallas kernels, body(): pl.pallas_call(kernel, out_shape=(jax.ShapeDtypeStruct((OWN, D), F32), ja...  90.9 us
    unnamed x2, local copies, waits for them, and re-layouts  2.95 us

profile of v1, /device:TPU:6, one launch (start us, length us, event | category | flops | bytes accessed | tf_op | source)
XLA Modules:
  0.0 95.8 jit_solution(14240130668983026668)
XLA Ops:
  0.6 1.3 %reshape.27.vrow = s32[1,1536]{1,0:T(1,128)} reshape(s32[1536]{0:T(1024)} %param.26) | data formatting | bytes 12288 | tf_op jit(solution)/shard_map/reshape | solution.py:521
  1.9 90.9 %shard_map.167 = (f32[32,512]{1,0:T(8,128)}, f32[32,512]{1,0:T(8,128)}) custom-call(bf16[256,512]{1,0:T(8,128)(2,1)} %msg.1, bf16[256,512]{1,0:T(8,128)(2,1)} %dst.1, bf16[1536,512]{1,0:T(8,128)(2,1)} %nbr.1, bf16[256,512]{1,0:T(8,128)(2,1)} %emb.1, s32[1,256]{1,0:T(1,128)} %bitcast.10, s32[6,256]{1,0:T(8,128)} %bitcast.8, s32[1,256]{1,0:T(1,128)} %bitcast.11, ...), custom_call_target="tpu_custom_call" | custom-call | flops 4000000000 | bytes 8000000 | tf_op jit(solution)/shard_map/pallas_call | solution.py:505
  92.9 1.5 %copy.20 = f32[32,512]{1,0:T(8,128)} copy(f32[32,512]{1,0:T(8,128)} %get-tuple-element.8) | data formatting | bytes 131072
  94.4 1.5 %copy.21 = f32[1,32,512]{2,1,0:T(8,128)} copy(f32[1,32,512]{2,1,0:T(8,128)} %bitcast.7) | data formatting | bytes 131072

commit v2 on v1

--- a/solution.py
+++ b/solution.py
@@ -1,4 +1,3 @@
-import functools
 import math
 
 import jax
@@ -57,7 +56,7 @@
     msg, dst, nbr, emb, ev_time, nb_time, nb_count, src_id, dst_loc, owner, vrow,
     w_in, w_hid, w_q, w_kv, w_out,
     ver_out, node_out,
-    wa, wb, rbuf, keys, gkb, qk, gv, ctx, gates, gmem, gin, gcand, gmsg, tcol, tpack, gwp, scp, wtp,
+    wa, wb, rbuf, keys, gkb, qk, gv, ctx, gates, mem, gmem, gin, gcand, gmsg, tcol, tpack, gwp, scp, wtp,
     vpart, vbuf, npart, nsib, nsend, nrecv, dpart,
     loc_sem, s1_send, s1_recv, r1_send, r2_send, piece_sem, sib_send, sib_recv,
     v_send, v_recv, nd_send, nd_recv, ring_send, ring_recv,
@@ -224,20 +223,36 @@
 
     lax.fori_loop(0, EV // 16, make_keys, 0)
 
+    step0(1)
     step0(0)
-    step0(1)
+    step1(1)
+    step2(1)
     step1(0)
     step2(0)
-    step1(1)
-    step2(1)
+    step3(1)
+    step4(1)
     step3(0)
-    step4(0)
-    step3(1)
-
-    all_here(0)
 
     def wide(ref, start, width):
         return ref[:, :, :, :, pl.ds(start, width)].reshape(D, width)
+
+    all_here(1)
+
+    def gate(k):
+        return (nn(msg[...], wide(wb, k * D, D)), nn(dst[...], wide(wb, 1536 + k * D, D)))
+
+    gi, gh = gate(0)
+    gates[0] = sigmoid(gi + gh)
+    gi, gh = gate(2)
+    gates[3] = gh
+    gates[2] = jnp.tanh(gi + gates[0] * gh)
+    gi, gh = gate(1)
+    update = sigmoid(gi + gh)
+    gates[1] = update
+    mem[...] = ((1.0 - update) * gates[2] + update * dst[...].astype(F32)).astype(BF16)
+
+    step4(0)
+    all_here(0)
 
     gatt = nt(emb[...], wide(wa, 1024, 512)).astype(BF16)
     for h in range(2):
@@ -262,23 +277,7 @@
 
     row_dots(gv, gwp)
 
-    step4(1)
-    all_here(1)
-
-    def gate(k):
-        return (nn(msg[...], wide(wb, k * D, D)), nn(dst[...], wide(wb, 1536 + k * D, D)))
-
-    gi, gh = gate(0)
-    reset = sigmoid(gi + gh)
-    gates[0] = reset
-    gi, gh = gate(2)
-    gates[3] = gh
-    gates[2] = jnp.tanh(gi + gates[0] * gh)
-    gi, gh = gate(1)
-    update = sigmoid(gi + gh)
-    gates[1] = update
-    memory = ((1.0 - update) * gates[2] + update * dst[...].astype(F32)).astype(BF16)
-    quer = nn(memory, wide(wa, 1536, 512)).astype(BF16)
+    quer = nn(mem[...], wide(wa, 1536, 512)).astype(BF16)
     for h in range(2):
         qk[h] = nt(quer[:, h * HEAD : (h + 1) * HEAD], wide(wa, h * HEAD, HEAD))
 
@@ -300,56 +299,20 @@
     wtp[...] = weight
     scp[...] = weight * (gw - per_head(weight * gw)) * (1.0 / 16.0)
 
-    def spread(i, carry):
+    def gather_slots(i, carry):
         at = pl.ds(pl.multiple_of(i * 16, 16), 16)
-        sc, wt = scp[at, :], wtp[at, :]
-        for lo in (0, 256):
-            cut = slice(lo, lo + 256)
-            q0, q1, g0, g1 = qk[0, at, cut], qk[1, at, cut], gv[0, at, cut], gv[1, at, cut]
-            c0 = jnp.zeros((16, 256), F32)
-            c1 = jnp.zeros((16, 256), F32)
-            for j in range(SLOTS):
-                s0, s1 = sc[:, j : j + 1], sc[:, SLOTS + j : SLOTS + j + 1]
-                w0, w1 = wt[:, j : j + 1], wt[:, SLOTS + j : SLOTS + j + 1]
-                key = keys[j, at, cut]
-                c0 = c0 + s0 * key
-                c1 = c1 + s1 * key
-                for half in range(0, 256, 128):
-                    hs = slice(half, half + 128)
-                    rbuf[(lo + half) // 128, pl.ds(i * (16 * SLOTS) + j, 16, stride=SLOTS), :] = (
-                        (s0 * q0[:, hs] + s1 * q1[:, hs]) + (w0 * g0[:, hs] + w1 * g1[:, hs])
-                    )
-            ctx[0, at, cut] = c0.astype(BF16)
-            ctx[1, at, cut] = c1.astype(BF16)
-        return carry
-
-    lax.fori_loop(0, EV // 16, spread, 0)
-
-    def narrow(i, carry):
-        at = pl.ds(pl.multiple_of(i * 64, 64), 64)
-        for t in range(4):
-            gkb[at, t * 128 : (t + 1) * 128] = rbuf[t, at, :].astype(BF16)
-        return carry
-
-    lax.fori_loop(0, READS // 64, narrow, 0)
-
-    vid = owner[...] * OWN + vrow[...]
-    for m in range(2):
-        hot = (lax.broadcasted_iota(jnp.int32, (256, READS), 0) + 256 * m == vid).astype(F32).astype(BF16)
-        sums = nn(hot, gkb[...]).astype(BF16)
-        vpart[pl.ds(8 * m, 8)] = sums.reshape(8, OWN, D)
-
-    def send_versions(k, carry):
-        to = (tm + k) % 16
-        pltpu.make_async_remote_copy(
-            src_ref=vpart.at[to], dst_ref=vbuf.at[k - 1],
-            send_sem=v_send, recv_sem=v_recv,
-            device_id=(to, node), device_id_type=MESH,
-        ).start()
-        return carry
-
-    lax.fori_loop(1, 16, send_versions, 0)
-
+        sc = scp[at, :]
+        c0 = jnp.zeros((16, D), F32)
+        c1 = jnp.zeros((16, D), F32)
+        for j in range(SLOTS):
+            key = keys[j, at, :]
+            c0 = c0 + sc[:, j : j + 1] * key
+            c1 = c1 + sc[:, SLOTS + j : SLOTS + j + 1] * key
+        ctx[0, at, :] = c0.astype(BF16)
+        ctx[1, at, :] = c1.astype(BF16)
+        return carry
+
+    lax.fori_loop(0, EV // 16, gather_slots, 0)
     gq = [nn(ctx[h], wide(wa, h * HEAD, HEAD)).astype(BF16) for h in range(2)]
     gmem[...] = emb[...].astype(F32) + (
         nt(gq[0], wide(wa, 1536, HEAD)) + nt(gq[1], wide(wa, 1536 + HEAD, HEAD))
@@ -373,9 +336,8 @@
     gmsg[...] = nt(gin[...], wide(wb, 0, 1536)).astype(BF16)
 
     def part_copy(g):
-        ref_from, ref_to = npart.at[g, other], nsib.at[g]
         return pltpu.make_async_remote_copy(
-            src_ref=ref_from, dst_ref=ref_to, send_sem=nd_send.at[g], recv_sem=nd_recv.at[g],
+            src_ref=npart.at[g, other], dst_ref=nsib.at[g], send_sem=nd_send.at[g], recv_sem=nd_recv.at[g],
             device_id=sibling, device_id_type=MESH,
         )
 
@@ -394,49 +356,97 @@
                 k = offsets.index(rel)
                 return npart[g, c, k].astype(F32) + nsib[g, k].astype(F32)
 
+    chains = (((8, 9, 10, 11), -1, -5), ((7, 6, 5), 1, 5), ((12, 13, 14, 15), -1, -1), ((4, 3, 2, 1), 1, 1))
+
     def hop(way, s):
-        to = (z + 15) % 16 if way == 0 else (z + 1) % 16
+        steps, near, last = chains[way]
+        to = (z + (last if s == len(steps) - 1 else near) + 16) % 16
         return pltpu.make_async_remote_copy(
             src_ref=nsend.at[way, s], dst_ref=nrecv.at[way, s],
             send_sem=ring_send.at[way, s], recv_sem=ring_recv.at[way, s],
             device_id=(tm, to * 2 + c), device_id_type=MESH,
         )
 
-    part_copy(0).wait()
-    nsend[0, 0] = mine(8).astype(BF16)
-    hop(0, 0).start()
-    nsend[1, 0] = mine(7).astype(BF16)
-    hop(1, 0).start()
+    def chain_step(way, s):
+        total = mine(chains[way][0][s])
+        if s > 0:
+            hop(way, s - 1).wait_recv()
+            total = total + nrecv[way, s - 1].astype(F32)
+        nsend[way, s] = total.astype(BF16)
+        hop(way, s).start()
+
+    def chain_steps(s):
+        for way in range(4):
+            if s < len(chains[way][0]):
+                chain_step(way, s)
+
+    def spread(i, carry):
+        at = pl.ds(pl.multiple_of(i * 16, 16), 16)
+        sc, wt = scp[at, :], wtp[at, :]
+        for j in range(SLOTS):
+            s0, s1 = sc[:, j : j + 1], sc[:, SLOTS + j : SLOTS + j + 1]
+            w0, w1 = wt[:, j : j + 1], wt[:, SLOTS + j : SLOTS + j + 1]
+            for t in range(4):
+                cut = slice(t * 128, (t + 1) * 128)
+                rbuf[t, pl.ds(i * (16 * SLOTS) + j, 16, stride=SLOTS), :] = (
+                    (s0 * qk[0, at, cut] + s1 * qk[1, at, cut]) + (w0 * gv[0, at, cut] + w1 * gv[1, at, cut])
+                )
+        return carry
+
+    def narrow(i, carry):
+        at = pl.ds(pl.multiple_of(i * 64, 64), 64)
+        for t in range(4):
+            gkb[at, t * 128 : (t + 1) * 128] = rbuf[t, at, :].astype(BF16)
+        return carry
+
+    def version_sums(m):
+        ids = []
+        for k in range(READS // 128):
+            vid = owner[:, k * 128 : (k + 1) * 128] * OWN + vrow[k : k + 1, :]
+            ids.append((lax.broadcasted_iota(jnp.int32, (256, 128), 0) + 256 * m == vid).astype(F32).astype(BF16))
+        sums = nn(jnp.concatenate(ids, axis=1), gkb[...]).astype(BF16)
+        vpart[pl.ds(8 * m, 8)] = sums.reshape(8, OWN, D)
+        for t in range(8 * m, 8 * m + 8):
+            @pl.when(tm != t)
+            def _(t=t):
+                pltpu.make_async_remote_copy(
+                    src_ref=vpart.at[t], dst_ref=vbuf.at[(t - tm + 15) % 16],
+                    send_sem=v_send, recv_sem=v_recv,
+                    device_id=(t, node), device_id_type=MESH,
+                ).start()
+
+    lax.fori_loop(0, EV // 32, spread, 0)
+    for g in range(3):
+        part_copy(g).wait()
+    chain_steps(0)
+    lax.fori_loop(EV // 32, EV // 16, spread, 0)
+    part_copy(3).wait()
+    chain_steps(1)
+    lax.fori_loop(0, READS // 64, narrow, 0)
+    version_sums(0)
+    chain_steps(2)
+    version_sums(1)
+    chain_steps(3)
 
     gdst = (nt(gin[:, 0:1024], wide(wb, 1536, 1024)) + nt(gcand[...], wide(wb, 2560, 512))) + gmem[...]
     hot = (lax.broadcasted_iota(jnp.int32, (OWN, EV), 0) == dst_loc[...]).astype(F32).astype(BF16)
-    dpart[...] = nn(hot, gdst.astype(BF16))
-
-    for g in range(1, 4):
-        part_copy(g).wait()
-
-    for s in range(1, 8):
-        hop(0, s - 1).wait_recv()
-        nsend[0, s] = (mine(8 + s) + nrecv[0, s - 1].astype(F32)).astype(BF16)
-        hop(0, s).start()
-        if s < 7:
-            hop(1, s - 1).wait_recv()
-            nsend[1, s] = (mine(7 - s) + nrecv[1, s - 1].astype(F32)).astype(BF16)
-            hop(1, s).start()
-        if s == 4:
-            pltpu.make_async_copy(vbuf, vbuf, v_recv).wait()
-            total = vpart[tm].astype(F32)
-            for k in range(15):
-                total = total + vbuf[k].astype(F32)
-            ver_out[...] = total
-    hop(0, 7).wait_recv()
-    hop(1, 6).wait_recv()
-    node_out[...] = (mine(0) + dpart[...]) + (nrecv[0, 7].astype(F32) + nrecv[1, 6].astype(F32))
-
-    for s in range(8):
-        hop(0, s).wait_send()
-        if s < 7:
-            hop(1, s).wait_send()
+    dpart[...] = mine(0) + nn(hot, gdst.astype(BF16))
+
+    ends = [(way, len(chains[way][0]) - 1) for way in range(4)]
+    for way, s in ends:
+        hop(way, s).wait_recv()
+    node_out[...] = dpart[...] + (
+        (nrecv[0, 3].astype(F32) + nrecv[1, 2].astype(F32)) + (nrecv[2, 3].astype(F32) + nrecv[3, 3].astype(F32))
+    )
+    pltpu.make_async_copy(vbuf, vbuf, v_recv).wait()
+    total = vpart[tm].astype(F32)
+    for k in range(15):
+        total = total + vbuf[k].astype(F32)
+    ver_out[...] = total
+
+    for way in range(4):
+        for s in range(len(chains[way][0])):
+            hop(way, s).wait_send()
     pltpu.make_async_copy(vbuf, vbuf, v_send).wait()
     for ph, (buf, width) in enumerate(bufs):
         ref = buf.at[:, :, c]
@@ -452,6 +462,17 @@
         pltpu.make_async_copy(ref, ref, s1_send.at[0]).wait()
         ref = wb.at[0, 0:3, :, :, 0:1920]
         pltpu.make_async_copy(ref, ref, s1_send.at[1]).wait()
+
+
+def hand_out(ver_in, node_in, ver_out, node_out, sems):
+    copies = [
+        pltpu.make_async_copy(ver_in, ver_out, sems.at[0]),
+        pltpu.make_async_copy(node_in, node_out, sems.at[1]),
+    ]
+    for copy in copies:
+        copy.start()
+    for copy in copies:
+        copy.wait()
 
 
 def body(
@@ -471,6 +492,7 @@
         pltpu.VMEM((2, EV, D), F32),
         pltpu.VMEM((2, EV, D), BF16),
         pltpu.VMEM((4, EV, D), F32),
+        pltpu.VMEM((EV, D), BF16),
         pltpu.VMEM((EV, D), F32),
         pltpu.VMEM((EV, 3 * D), BF16),
         pltpu.VMEM((EV, D), BF16),
@@ -484,8 +506,8 @@
         pltpu.VMEM((15, OWN, D), BF16),
         pltpu.VMEM((4, 2, 4, OWN, D), BF16),
         pltpu.VMEM((4, 4, OWN, D), BF16),
-        pltpu.VMEM((2, 8, OWN, D), BF16),
-        pltpu.VMEM((2, 8, OWN, D), BF16),
+        pltpu.VMEM((4, 4, OWN, D), BF16),
+        pltpu.VMEM((4, 4, OWN, D), BF16),
         pltpu.VMEM((OWN, D), F32),
         dma((2,)),
         dma((2,)),
@@ -499,8 +521,8 @@
         dma,
         dma((4,)),
         dma((4,)),
-        dma((2, 8)),
-        dma((2, 8)),
+        dma((4, 4)),
+        dma((4, 4)),
     ]
     version_grad, node_grad = pl.pallas_call(
         kernel,
@@ -518,9 +540,17 @@
         message, dest_mem, nbr_rows, emb_grad,
         event_time.reshape(1, EV), nbr_time.T, nbr_count.reshape(1, EV),
         source_id.reshape(1, EV), dest_local.reshape(1, EV),
-        read_owner.reshape(1, READS), read_row.reshape(1, READS),
+        read_owner.reshape(1, READS), read_row.reshape(READS // 128, 128),
         w_in, w_hid, w_query, w_keyval, w_out,
     )
+    version_grad, node_grad = pl.pallas_call(
+        hand_out,
+        out_shape=(jax.ShapeDtypeStruct((OWN, D), F32), jax.ShapeDtypeStruct((OWN, D), F32)),
+        in_specs=[hbm] * 2,
+        out_specs=(hbm, hbm),
+        scratch_shapes=[dma((2,))],
+        compiler_params=pltpu.CompilerParams(vmem_limit_bytes=60 * 1024 * 1024),
+    )(version_grad, node_grad)
     return version_grad, node_grad[None]
 
 

time: 96.2 us -> 90.8 us (0.944)
  local copies, waits for them, and re-layouts: 4.24 us -> 0 us
  Pallas kernels: 90.9 us -> 89.7 us
    pallas_call x1, Pallas kernels: 90.9 us -> 84.6 us  [body(): pl.pallas_call(kernel, out_shape=(jax.ShapeDtypeStruct((OWN, D), F32), ja...]
    pallas_call x0 -> x1, Pallas kernels: none -> 5.09 us  [body(): pl.pallas_call(hand_out, out_shape=(jax.ShapeDtypeStruct((OWN, D), F32),...]
    unnamed x2 -> x0, local copies, waits for them, and re-layouts: 2.95 us -> none
    reshape x1 -> x0, local copies, waits for them, and re-layouts: 1.3 us -> none  [body(): read_row.reshape(1, READS)]
where the time goes in v2:
time: 90.8 us; the launch traced here: 90.3 us
  Pallas kernels  89.7 us (99%)
    pallas_call x1, Pallas kernels, body(): pl.pallas_call(kernel, out_shape=(jax.ShapeDtypeStruct((OWN, D), F32), ja...  84.6 us
    pallas_call x1, Pallas kernels, body(): pl.pallas_call(hand_out, out_shape=(jax.ShapeDtypeStruct((OWN, D), F32),...  5.09 us

profile of v2, /device:TPU:6, one launch (start us, length us, event | category | flops | bytes accessed | tf_op | source)
XLA Modules:
  0.0 90.3 jit_solution(11359995100255483209)
XLA Ops:
  0.6 84.6 %shard_map.167 = (f32[32,512]{1,0:T(8,128)}, f32[32,512]{1,0:T(8,128)}) custom-call(bf16[256,512]{1,0:T(8,128)(2,1)} %msg.1, bf16[256,512]{1,0:T(8,128)(2,1)} %dst.1, bf16[1536,512]{1,0:T(8,128)(2,1)} %nbr.1, bf16[256,512]{1,0:T(8,128)(2,1)} %emb.1, s32[1,256]{1,0:T(1,128)} %bitcast.12, s32[6,256]{1,0:T(8,128)} %bitcast.9, s32[1,256]{1,0:T(1,128)} %bitcast.13, ...), custom_call_target="tpu_custom_call" | custom-call | flops 4000000000 | bytes 8000000 | tf_op jit(solution)/shard_map/pallas_call | solution.py:527
  85.2 5.1 %shard_map.168 = (f32[32,512]{1,0:T(8,128)}, f32[32,512]{1,0:T(8,128)}) custom-call(f32[32,512]{1,0:T(8,128)} %get-tuple-element.6.ver_in, f32[32,512]{1,0:T(8,128)} %get-tuple-element.7.node_in), custom_call_target="tpu_custom_call" | custom-call | tf_op jit(solution)/shard_map/pallas_call | solution.py:546

commit v3 on v2

--- a/solution.py
+++ b/solution.py
@@ -52,14 +52,11 @@
     return 1.0 + q * (q * (1.0 / 24.0) - 0.5)
 
 
-def kernel(
-    msg, dst, nbr, emb, ev_time, nb_time, nb_count, src_id, dst_loc, owner, vrow,
-    w_in, w_hid, w_q, w_kv, w_out,
-    ver_out, node_out,
-    wa, wb, rbuf, keys, gkb, qk, gv, ctx, gates, mem, gmem, gin, gcand, gmsg, tcol, tpack, gwp, scp, wtp,
-    vpart, vbuf, npart, nsib, nsend, nrecv, dpart,
+def gather_kernel(
+    nbr, ev_time, nb_time, nb_count, w_in, w_hid, w_q, w_kv, w_out,
+    wa, wb, keys, tcol,
+    rbuf, tpack,
     loc_sem, s1_send, s1_recv, r1_send, r2_send, piece_sem, sib_send, sib_recv,
-    v_send, v_recv, nd_send, nd_recv, ring_send, ring_recv,
 ):
     tm = lax.axis_index("tm")
     node = lax.axis_index("node")
@@ -232,11 +229,35 @@
     step3(1)
     step4(1)
     step3(0)
+    step4(0)
+    all_here(1)
+    all_here(0)
+
+    for ph, (buf, width) in enumerate(bufs):
+        ref = buf.at[:, :, c]
+        pltpu.make_async_copy(ref, ref, sib_send.at[ph]).wait()
+        ref = buf.at[:, 0:3, c, :, 0:width]
+        pltpu.make_async_copy(ref, ref, r1_send.at[ph]).wait()
+        ref = buf.at[:, 0:3, c]
+        pltpu.make_async_copy(ref, ref, r2_send.at[ph]).wait()
+
+    @pl.when(zy == y)
+    def _():
+        ref = wa.at[:, 0, c, :, 0:1920]
+        pltpu.make_async_copy(ref, ref, s1_send.at[0]).wait()
+        ref = wb.at[0, 0:3, :, :, 0:1920]
+        pltpu.make_async_copy(ref, ref, s1_send.at[1]).wait()
+
+
+def math_kernel(
+    msg, dst, emb, wa, wb, keys, tcol, src_id, dst_loc, owner, vrow,
+    vpart, npart, dpart,
+    rbuf, gkb, qk, gv, ctx, gates, mem, gmem, gin, gcand, gmsg, gwp, scp, wtp,
+):
+    z = lax.axis_index("node") // 2
 
     def wide(ref, start, width):
         return ref[:, :, :, :, pl.ds(start, width)].reshape(D, width)
-
-    all_here(1)
 
     def gate(k):
         return (nn(msg[...], wide(wb, k * D, D)), nn(dst[...], wide(wb, 1536 + k * D, D)))
@@ -250,9 +271,6 @@
     update = sigmoid(gi + gh)
     gates[1] = update
     mem[...] = ((1.0 - update) * gates[2] + update * dst[...].astype(F32)).astype(BF16)
-
-    step4(0)
-    all_here(0)
 
     gatt = nt(emb[...], wide(wa, 1024, 512)).astype(BF16)
     for h in range(2):
@@ -335,12 +353,6 @@
 
     gmsg[...] = nt(gin[...], wide(wb, 0, 1536)).astype(BF16)
 
-    def part_copy(g):
-        return pltpu.make_async_remote_copy(
-            src_ref=npart.at[g, other], dst_ref=nsib.at[g], send_sem=nd_send.at[g], recv_sem=nd_recv.at[g],
-            device_id=sibling, device_id_type=MESH,
-        )
-
     for g, offsets in enumerate(FAR):
         base = ((z + offsets[0]) % 16) * 64
         wanted = (lax.broadcasted_iota(jnp.int32, (256, EV), 0) + base) & 1023
@@ -348,37 +360,6 @@
         sums = nn(hot, gmsg[...]).astype(BF16).reshape(4, 2, OWN, D)
         npart[g, 0] = sums[:, 0]
         npart[g, 1] = sums[:, 1]
-        part_copy(g).start()
-
-    def mine(rel):
-        for g, offsets in enumerate(FAR):
-            if rel in offsets:
-                k = offsets.index(rel)
-                return npart[g, c, k].astype(F32) + nsib[g, k].astype(F32)
-
-    chains = (((8, 9, 10, 11), -1, -5), ((7, 6, 5), 1, 5), ((12, 13, 14, 15), -1, -1), ((4, 3, 2, 1), 1, 1))
-
-    def hop(way, s):
-        steps, near, last = chains[way]
-        to = (z + (last if s == len(steps) - 1 else near) + 16) % 16
-        return pltpu.make_async_remote_copy(
-            src_ref=nsend.at[way, s], dst_ref=nrecv.at[way, s],
-            send_sem=ring_send.at[way, s], recv_sem=ring_recv.at[way, s],
-            device_id=(tm, to * 2 + c), device_id_type=MESH,
-        )
-
-    def chain_step(way, s):
-        total = mine(chains[way][0][s])
-        if s > 0:
-            hop(way, s - 1).wait_recv()
-            total = total + nrecv[way, s - 1].astype(F32)
-        nsend[way, s] = total.astype(BF16)
-        hop(way, s).start()
-
-    def chain_steps(s):
-        for way in range(4):
-            if s < len(chains[way][0]):
-                chain_step(way, s)
 
     def spread(i, carry):
         at = pl.ds(pl.multiple_of(i * 16, 16), 16)
@@ -406,36 +387,98 @@
             ids.append((lax.broadcasted_iota(jnp.int32, (256, 128), 0) + 256 * m == vid).astype(F32).astype(BF16))
         sums = nn(jnp.concatenate(ids, axis=1), gkb[...]).astype(BF16)
         vpart[pl.ds(8 * m, 8)] = sums.reshape(8, OWN, D)
-        for t in range(8 * m, 8 * m + 8):
-            @pl.when(tm != t)
-            def _(t=t):
-                pltpu.make_async_remote_copy(
-                    src_ref=vpart.at[t], dst_ref=vbuf.at[(t - tm + 15) % 16],
-                    send_sem=v_send, recv_sem=v_recv,
-                    device_id=(t, node), device_id_type=MESH,
-                ).start()
-
-    lax.fori_loop(0, EV // 32, spread, 0)
+
+    lax.fori_loop(0, EV // 16, spread, 0)
+    lax.fori_loop(0, READS // 64, narrow, 0)
+    version_sums(0)
+    version_sums(1)
+    gdst = (nt(gin[:, 0:1024], wide(wb, 1536, 1024)) + nt(gcand[...], wide(wb, 2560, 512))) + gmem[...]
+    hot = (lax.broadcasted_iota(jnp.int32, (OWN, EV), 0) == dst_loc[...]).astype(F32).astype(BF16)
+    dpart[...] = nn(hot, gdst.astype(BF16))
+
+
+def sums_kernel(
+    vpart, npart, dpart,
+    ver_out, node_out,
+    vbuf, nsib, nsend, nrecv,
+    v_send, v_recv, nd_send, nd_recv, ring_send, ring_recv,
+):
+    tm = lax.axis_index("tm")
+    node = lax.axis_index("node")
+    z, c = node // 2, node % 2
+    other = 1 - c
+    sibling = (tm, z * 2 + other)
+
+    barrier = pltpu.get_barrier_semaphore()
+
+    def greet(k, carry):
+        pl.semaphore_signal(barrier, inc=1, device_id=(tm, (node + 2 * k) % 32), device_id_type=MESH)
+        pl.semaphore_signal(barrier, inc=1, device_id=((tm + k) % 16, node), device_id_type=MESH)
+        return carry
+
+    lax.fori_loop(1, 16, greet, 0)
+    pl.semaphore_signal(barrier, inc=1, device_id=sibling, device_id_type=MESH)
+    pl.semaphore_wait(barrier, 31)
+
+    def part_copy(g):
+        return pltpu.make_async_remote_copy(
+            src_ref=npart.at[g, other], dst_ref=nsib.at[g], send_sem=nd_send.at[g], recv_sem=nd_recv.at[g],
+            device_id=sibling, device_id_type=MESH,
+        )
+
+    def mine(rel):
+        for g, offsets in enumerate(FAR):
+            if rel in offsets:
+                k = offsets.index(rel)
+                return npart[g, c, k].astype(F32) + nsib[g, k].astype(F32)
+
+    chains = (((8, 9, 10, 11), -1, -5), ((7, 6, 5), 1, 5), ((12, 13, 14, 15), -1, -1), ((4, 3, 2, 1), 1, 1))
+
+    def hop(way, s):
+        steps, near, last = chains[way]
+        to = (z + (last if s == len(steps) - 1 else near) + 16) % 16
+        return pltpu.make_async_remote_copy(
+            src_ref=nsend.at[way, s], dst_ref=nrecv.at[way, s],
+            send_sem=ring_send.at[way, s], recv_sem=ring_recv.at[way, s],
+            device_id=(tm, to * 2 + c), device_id_type=MESH,
+        )
+
+    def chain_step(way, s):
+        total = mine(chains[way][0][s])
+        if s > 0:
+            hop(way, s - 1).wait_recv()
+            total = total + nrecv[way, s - 1].astype(F32)
+        nsend[way, s] = total.astype(BF16)
+        hop(way, s).start()
+
+    def chain_steps(s):
+        for way in range(4):
+            if s < len(chains[way][0]):
+                chain_step(way, s)
+
+    def send_versions(k, carry):
+        to = (tm + k) % 16
+        pltpu.make_async_remote_copy(
+            src_ref=vpart.at[to], dst_ref=vbuf.at[k - 1],
+            send_sem=v_send, recv_sem=v_recv,
+            device_id=(to, node), device_id_type=MESH,
+        ).start()
+        return carry
+
+    for g in range(4):
+        part_copy(g).start()
+    lax.fori_loop(1, 16, send_versions, 0)
     for g in range(3):
         part_copy(g).wait()
     chain_steps(0)
-    lax.fori_loop(EV // 32, EV // 16, spread, 0)
     part_copy(3).wait()
-    chain_steps(1)
-    lax.fori_loop(0, READS // 64, narrow, 0)
-    version_sums(0)
-    chain_steps(2)
-    version_sums(1)
-    chain_steps(3)
-
-    gdst = (nt(gin[:, 0:1024], wide(wb, 1536, 1024)) + nt(gcand[...], wide(wb, 2560, 512))) + gmem[...]
-    hot = (lax.broadcasted_iota(jnp.int32, (OWN, EV), 0) == dst_loc[...]).astype(F32).astype(BF16)
-    dpart[...] = mine(0) + nn(hot, gdst.astype(BF16))
+    for s in range(1, 4):
+        chain_steps(s)
 
     ends = [(way, len(chains[way][0]) - 1) for way in range(4)]
     for way, s in ends:
         hop(way, s).wait_recv()
-    node_out[...] = dpart[...] + (
+    node_out[...] = (mine(0) + dpart[...]) + (
         (nrecv[0, 3].astype(F32) + nrecv[1, 2].astype(F32)) + (nrecv[2, 3].astype(F32) + nrecv[3, 3].astype(F32))
     )
     pltpu.make_async_copy(vbuf, vbuf, v_recv).wait()
@@ -448,31 +491,6 @@
         for s in range(len(chains[way][0])):
             hop(way, s).wait_send()
     pltpu.make_async_copy(vbuf, vbuf, v_send).wait()
-    for ph, (buf, width) in enumerate(bufs):
-        ref = buf.at[:, :, c]
-        pltpu.make_async_copy(ref, ref, sib_send.at[ph]).wait()
-        ref = buf.at[:, 0:3, c, :, 0:width]
-        pltpu.make_async_copy(ref, ref, r1_send.at[ph]).wait()
-        ref = buf.at[:, 0:3, c]
-        pltpu.make_async_copy(ref, ref, r2_send.at[ph]).wait()
-
-    @pl.when(zy == y)
-    def _():
-        ref = wa.at[:, 0, c, :, 0:1920]
-        pltpu.make_async_copy(ref, ref, s1_send.at[0]).wait()
-        ref = wb.at[0, 0:3, :, :, 0:1920]
-        pltpu.make_async_copy(ref, ref, s1_send.at[1]).wait()
-
-
-def hand_out(ver_in, node_in, ver_out, node_out, sems):
-    copies = [
-        pltpu.make_async_copy(ver_in, ver_out, sems.at[0]),
-        pltpu.make_async_copy(node_in, node_out, sems.at[1]),
-    ]
-    for copy in copies:
-        copy.start()
-    for copy in copies:
-        copy.wait()
 
 
 def body(
@@ -482,75 +500,75 @@
     vmem = pl.BlockSpec(memory_space=pltpu.VMEM)
     hbm = pl.BlockSpec(memory_space=pl.ANY)
     dma = pltpu.SemaphoreType.DMA
-    scratch = [
-        pltpu.VMEM((4, 4, 2, 16, 2048), BF16),
-        pltpu.VMEM((4, 4, 2, 16, 3072), BF16),
-        pltpu.VMEM((4, READS, 128), F32),
-        pltpu.VMEM((SLOTS, EV, D), F32),
-        pltpu.VMEM((READS, D), BF16),
-        pltpu.VMEM((2, EV, D), F32),
-        pltpu.VMEM((2, EV, D), F32),
-        pltpu.VMEM((2, EV, D), BF16),
-        pltpu.VMEM((4, EV, D), F32),
-        pltpu.VMEM((EV, D), BF16),
-        pltpu.VMEM((EV, D), F32),
-        pltpu.VMEM((EV, 3 * D), BF16),
-        pltpu.VMEM((EV, D), BF16),
-        pltpu.VMEM((EV, D), BF16),
-        pltpu.VMEM((EV, 8), F32),
-        pltpu.VMEM((8, EV), F32),
-        pltpu.VMEM((EV, 128), F32),
-        pltpu.VMEM((EV, 128), F32),
-        pltpu.VMEM((EV, 128), F32),
-        pltpu.VMEM((16, OWN, D), BF16),
-        pltpu.VMEM((15, OWN, D), BF16),
-        pltpu.VMEM((4, 2, 4, OWN, D), BF16),
-        pltpu.VMEM((4, 4, OWN, D), BF16),
-        pltpu.VMEM((4, 4, OWN, D), BF16),
-        pltpu.VMEM((4, 4, OWN, D), BF16),
-        pltpu.VMEM((OWN, D), F32),
-        dma((2,)),
-        dma((2,)),
-        dma((2, 4)),
-        dma((2,)),
-        dma((2,)),
-        dma((2, 16, 2)),
-        dma((2,)),
-        dma((2,)),
-        dma,
-        dma,
-        dma((4,)),
-        dma((4,)),
-        dma((4, 4)),
-        dma((4, 4)),
-    ]
-    version_grad, node_grad = pl.pallas_call(
-        kernel,
-        out_shape=(jax.ShapeDtypeStruct((OWN, D), F32), jax.ShapeDtypeStruct((OWN, D), F32)),
-        in_specs=[vmem] * 11 + [hbm] * 5,
-        out_specs=(vmem, vmem),
-        scratch_shapes=scratch,
+    shape = jax.ShapeDtypeStruct
+    wa, wb, keys, tcol = pl.pallas_call(
+        gather_kernel,
+        out_shape=(
+            shape((4, 4, 2, 16, 2048), BF16), shape((4, 4, 2, 16, 3072), BF16),
+            shape((SLOTS, EV, D), F32), shape((EV, 8), F32),
+        ),
+        in_specs=[vmem] * 4 + [hbm] * 5,
+        out_specs=(vmem,) * 4,
+        scratch_shapes=[
+            pltpu.VMEM((4, READS, 128), F32),
+            pltpu.VMEM((8, EV), F32),
+            dma((2,)), dma((2,)), dma((2, 4)), dma((2,)), dma((2,)), dma((2, 16, 2)), dma((2,)), dma((2,)),
+        ],
         compiler_params=pltpu.CompilerParams(
-            collective_id=0, has_side_effects=True, vmem_limit_bytes=56 * 1024 * 1024
+            collective_id=0, has_side_effects=True, vmem_limit_bytes=24 * 1024 * 1024
         ),
+        cost_estimate=pl.CostEstimate(flops=20_000_000, bytes_accessed=8_000_000, transcendentals=0),
+    )(
+        nbr_rows, event_time.reshape(1, EV), nbr_time.T, nbr_count.reshape(1, EV),
+        w_in, w_hid, w_query, w_keyval, w_out,
+    )
+    vpart, npart, dpart = pl.pallas_call(
+        math_kernel,
+        out_shape=(shape((16, OWN, D), BF16), shape((4, 2, 4, OWN, D), BF16), shape((OWN, D), F32)),
+        in_specs=[vmem] * 11,
+        out_specs=(vmem,) * 3,
+        scratch_shapes=[
+            pltpu.VMEM((4, READS, 128), F32),
+            pltpu.VMEM((READS, D), BF16),
+            pltpu.VMEM((2, EV, D), F32),
+            pltpu.VMEM((2, EV, D), F32),
+            pltpu.VMEM((2, EV, D), BF16),
+            pltpu.VMEM((4, EV, D), F32),
+            pltpu.VMEM((EV, D), BF16),
+            pltpu.VMEM((EV, D), F32),
+            pltpu.VMEM((EV, 3 * D), BF16),
+            pltpu.VMEM((EV, D), BF16),
+            pltpu.VMEM((EV, D), BF16),
+            pltpu.VMEM((EV, 128), F32),
+            pltpu.VMEM((EV, 128), F32),
+            pltpu.VMEM((EV, 128), F32),
+        ],
+        compiler_params=pltpu.CompilerParams(vmem_limit_bytes=40 * 1024 * 1024),
         cost_estimate=pl.CostEstimate(
             flops=4_000_000_000, bytes_accessed=8_000_000, transcendentals=1_000_000
         ),
     )(
-        message, dest_mem, nbr_rows, emb_grad,
-        event_time.reshape(1, EV), nbr_time.T, nbr_count.reshape(1, EV),
+        message, dest_mem, emb_grad, wa, wb, keys, tcol,
         source_id.reshape(1, EV), dest_local.reshape(1, EV),
         read_owner.reshape(1, READS), read_row.reshape(READS // 128, 128),
-        w_in, w_hid, w_query, w_keyval, w_out,
     )
     version_grad, node_grad = pl.pallas_call(
-        hand_out,
-        out_shape=(jax.ShapeDtypeStruct((OWN, D), F32), jax.ShapeDtypeStruct((OWN, D), F32)),
-        in_specs=[hbm] * 2,
-        out_specs=(hbm, hbm),
-        scratch_shapes=[dma((2,))],
-        compiler_params=pltpu.CompilerParams(vmem_limit_bytes=60 * 1024 * 1024),
-    )(version_grad, node_grad)
+        sums_kernel,
+        out_shape=(shape((OWN, D), F32), shape((OWN, D), F32)),
+        in_specs=[vmem] * 3,
+        out_specs=(vmem,) * 2,
+        scratch_shapes=[
+            pltpu.VMEM((15, OWN, D), BF16),
+            pltpu.VMEM((4, 4, OWN, D), BF16),
+            pltpu.VMEM((4, 4, OWN, D), BF16),
+            pltpu.VMEM((4, 4, OWN, D), BF16),
+            dma, dma, dma((4,)), dma((4,)), dma((4, 4)), dma((4, 4)),
+        ],
+        compiler_params=pltpu.CompilerParams(
+            collective_id=1, has_side_effects=True, vmem_limit_bytes=24 * 1024 * 1024
+        ),
+        cost_estimate=pl.CostEstimate(flops=10_000_000, bytes_accessed=2_000_000, transcendentals=0),
+    )(vpart, npart, dpart)
     return version_grad, node_grad[None]
 
 

time: 90.8 us -> 109 us (1.20)
  local copies, waits for them, and re-layouts: 0 us -> 14.1 us
  Pallas kernels: 89.7 us -> 93.1 us
    unnamed x0 -> x34, local copies, waits for them, and re-layouts: none -> 14.1 us
    pallas_call x2 -> x3, Pallas kernels: 89.7 us -> 93.1 us  [the longest x1 54.2 us: body(): pl.pallas_call(gather_kernel, out_shape=(shape((4, 4, 2, 16, 2048), BF16)...]
where the time goes in v3:
time: 109 us; the launch traced here: 108 us
  Pallas kernels  93.1 us (85%)
  local copies, waits for them, and re-layouts  14.1 us (13%)
    pallas_call x1, Pallas kernels, body(): pl.pallas_call(gather_kernel, out_shape=(shape((4, 4, 2, 16, 2048), BF16)...  54.2 us
    pallas_call x1, Pallas kernels, body(): pl.pallas_call(sums_kernel, out_shape=(shape((OWN, D), F32), shape((OWN,...  25.5 us
    unnamed x34, local copies, waits for them, and re-layouts  14.1 us
    pallas_call x1, Pallas kernels, body(): pl.pallas_call(math_kernel, out_shape=(shape((16, OWN, D), BF16), shape((...  13.4 us

profile of v3, /device:TPU:6, one launch (start us, length us, event | category | flops | bytes accessed | tf_op | source)
XLA Modules:
  0.0 107.9 jit_solution(17182867312790023413)
XLA Ops:
  0.6 0.0 copy-start
  0.6 1.4 %copy-done = bf16[1536,512]{1,0:T(8,128)(2,1)S(1)} copy-done((bf16[1536,512]{1,0:T(8,128)(2,1)S(1)}, bf16[1536,512]{1,0:T(8,128)(2,1)}, u32[]{:S(2)}) %copy-start) | copy-done | bytes 1572888
  2.0 0.0 copy-start.1
  2.0 0.8 copy-done.1
  2.8 0.0 copy-start.2
  2.8 0.8 copy-done.2
  3.6 0.0 copy-start.3
  3.6 0.8 copy-done.3
  4.4 0.0 copy-start.4
  4.4 0.7 copy-done.4
  5.1 0.0 copy-start.5
  5.1 0.7 copy-done.5
  5.8 0.7 copy-done.6
  6.5 0.0 copy-start.7
  6.5 0.7 copy-done.7
  7.2 0.0 copy-start.8
  7.2 0.7 copy-done.8
  7.9 54.2 %shard_map.167 = (bf16[4,4,2,16,2048]{4,3,2,1,0:T(8,128)(2,1)S(1)}, bf16[4,4,2,16,3072]{4,3,2,1,0:T(8,128)(2,1)S(1)}, f32[6,256,512]{2,1,0:T(8,128)S(1)}, f32[256,8]{1,0:T(8,128)S(1)}) custom-call(bf16[1536,512]{1,0:T(8,128)(2,1)S(1)} %copy-done, s32[1,256]{1,0:T(1,128)S(1)} %bitcast.10, s32[6,256]{1,0:T(8,128)S(1)} %bitcast.9, s32[1,256]{1,0:T(1,128)S(1)} %bitcast.11, ...), custom_call_target="tpu_custom_call" | custom-call | flops 20000000 | bytes 8000000 | tf_op jit(solution)/shard_map/pallas_call | solution.py:504
  62.1 0.0 copy-start.9
  62.1 0.9 copy-done.9
  63.0 0.0 copy-start.10
  63.0 0.9 copy-done.10
  64.0 0.9 copy-done.11
  64.9 0.0 copy-start.12
  64.9 0.7 copy-done.12
  65.6 0.7 copy-done.13
  66.3 0.7 copy-done.14
  67.0 0.7 copy-done.15
  67.7 13.4 %shard_map.168 = (bf16[16,32,512]{2,1,0:T(8,128)(2,1)S(1)}, bf16[4,2,4,32,512]{4,3,2,1,0:T(8,128)(2,1)S(1)}, f32[32,512]{1,0:T(8,128)S(1)}) custom-call(bf16[256,512]{1,0:T(8,128)(2,1)S(1)} %copy-done.9, bf16[256,512]{1,0:T(8,128)(2,1)S(1)} %copy-done.10, bf16[256,512]{1,0:T(8,128)(2,1)S(1)} %copy-done.11, ...), custom_call_target="tpu_custom_call" | custom-call | flops 4000000000 | bytes 8000000 | tf_op jit(solution)/shard_map/pallas_call | solution.py:525
  81.1 25.5 %shard_map.169 = (f32[32,512]{1,0:T(8,128)S(1)}, f32[32,512]{1,0:T(8,128)S(1)}) custom-call(bf16[16,32,512]{2,1,0:T(8,128)(2,1)S(1)} %get-tuple-element.15.vpart, bf16[4,2,4,32,512]{4,3,2,1,0:T(8,128)(2,1)S(1)} %get-tuple-element.16.npart, f32[32,512]{1,0:T(8,128)S(1)} %get-tuple-element.17.dpart), custom_call_target="tpu_custom_call" | custom-call | flops 10000000 | bytes 2000000 | tf_op jit(solution)/shard_map/pallas_call | solution.py:555
  106.6 0.6 copy.20
  107.3 0.6 copy.21
  (5 shorter events, 0.0 us)
Async XLA Ops:
  0.6 1.4 %copy-start = (bf16[1536,512]{1,0:T(8,128)(2,1)S(1)}, bf16[1536,512]{1,0:T(8,128)(2,1)}, u32[]{:S(2)}) copy-start(bf16[1536,512]{1,0:T(8,128)(2,1)} %nbr.1) | copy-start | bytes 4718596
  2.0 0.8 copy-start.1
  2.8 0.8 copy-start.2
  3.6 0.8 copy-start.3
  4.4 0.7 copy-start.4
  5.1 0.7 copy-start.5
  5.8 0.7 copy-start.6
  6.5 0.7 copy-start.7
  7.2 0.7 copy-start.8
  62.1 1.0 copy-start.9
  63.0 0.9 copy-start.10
  64.0 0.9 copy-start.11
  64.9 0.7 copy-start.12
  65.6 0.7 copy-start.13
  66.3 0.7 copy-start.14
  67.0 0.7 copy-start.15

commit v4 on v2

--- a/solution.py
+++ b/solution.py
@@ -112,7 +112,8 @@
     @pl.when(zy == y)
     def _():
         for ph in range(2):
-            def send(k, carry, ph=ph):
+            def send(i, carry, ph=ph):
+                k = jnp.where(i % 2 == 0, 8 - i // 2, 8 + (i + 1) // 2)
                 pltpu.make_async_remote_copy(
                     src_ref=share(ph, zq), dst_ref=share(ph, zq),
                     send_sem=s1_send.at[ph], recv_sem=s1_recv.at[ph, zq],
@@ -120,7 +121,7 @@
                 ).start()
                 return carry
             pltpu.make_async_copy(share(ph, zq), share(ph, zq), loc_sem.at[ph]).wait()
-            lax.fori_loop(1, 16, send, 0)
+            lax.fori_loop(0, 15, send, 0)
 
     def stage1_wait(ph):
         for q in range(4):
@@ -146,17 +147,26 @@
         ref = piece(ph, aa, bb, part)
         pltpu.make_async_copy(ref, ref, piece_sem.at[ph, aa * 4 + bb, slot]).wait()
 
-    def to_sibling(ph, aa, bb):
-        ref = piece(ph, aa, bb)
-        pltpu.make_async_remote_copy(
-            src_ref=ref, dst_ref=ref, send_sem=sib_send.at[ph], recv_sem=sib_recv.at[ph],
-            device_id=sibling, device_id_type=MESH,
-        ).start()
+    def to_sibling(ph, bb):
+        buf, width = bufs[ph]
+
+        def send(ref):
+            pltpu.make_async_remote_copy(
+                src_ref=ref, dst_ref=ref, send_sem=sib_send.at[ph], recv_sem=sib_recv.at[ph],
+                device_id=sibling, device_id_type=MESH,
+            ).start()
+
+        @pl.when(c == 0)
+        def _():
+            send(buf.at[:, bb, 0])
+
+        @pl.when(c == 1)
+        def _():
+            send(buf.at[:, :, 1, :, pl.ds(pl.multiple_of(bb * width, 128), width)])
 
     def second_ring(ph, aa):
         send_piece(ph, aa, b, dev_b_left, r2_send)
         send_piece(ph, aa, b, dev_b_right, r2_send)
-        to_sibling(ph, aa, b)
 
     def step0(ph):
         stage1_wait(ph)
@@ -176,21 +186,22 @@
         wait_piece(ph, a_far, b, 0, 0)
         wait_piece(ph, a_far, b, 1, 1)
         second_ring(ph, a_far)
+        to_sibling(ph, b)
 
     def step3(ph):
         for aa in (a, a_left, a_right, a_far):
             wait_piece(ph, aa, b_left)
             send_piece(ph, aa, b_left, dev_b_right, r2_send, 0, 0)
-            to_sibling(ph, aa, b_left)
             wait_piece(ph, aa, b_right)
             send_piece(ph, aa, b_right, dev_b_left, r2_send, 1, 1)
-            to_sibling(ph, aa, b_right)
+        to_sibling(ph, b_left)
+        to_sibling(ph, b_right)
 
     def step4(ph):
         for aa in (a, a_left, a_right, a_far):
             wait_piece(ph, aa, b_far, 0, 0)
             wait_piece(ph, aa, b_far, 1, 1)
-            to_sibling(ph, aa, b_far)
+        to_sibling(ph, b_far)
 
     def all_here(ph):
         ref = bufs[ph][0].at[:, :, other]
@@ -464,15 +475,9 @@
         pltpu.make_async_copy(ref, ref, s1_send.at[1]).wait()
 
 
-def hand_out(ver_in, node_in, ver_out, node_out, sems):
-    copies = [
-        pltpu.make_async_copy(ver_in, ver_out, sems.at[0]),
-        pltpu.make_async_copy(node_in, node_out, sems.at[1]),
-    ]
-    for copy in copies:
-        copy.start()
-    for copy in copies:
-        copy.wait()
+def hand_out(ver_in, node_in, ver_out, node_out):
+    ver_out[...] = ver_in[...]
+    node_out[...] = node_in[...]
 
 
 def body(
@@ -546,9 +551,8 @@
     version_grad, node_grad = pl.pallas_call(
         hand_out,
         out_shape=(jax.ShapeDtypeStruct((OWN, D), F32), jax.ShapeDtypeStruct((OWN, D), F32)),
-        in_specs=[hbm] * 2,
-        out_specs=(hbm, hbm),
-        scratch_shapes=[dma((2,))],
+        in_specs=[vmem] * 2,
+        out_specs=(vmem, vmem),
         compiler_params=pltpu.CompilerParams(vmem_limit_bytes=60 * 1024 * 1024),
     )(version_grad, node_grad)
     return version_grad, node_grad[None]

time: 90.8 us -> 84.9 us (0.935); the launches traced: 90.3 us -> 83.5 us
  Pallas kernels: 89.7 us -> 82.8 us
    pallas_call x1, Pallas kernels: 5.09 us -> 1.53 us  [body(): pl.pallas_call(hand_out, out_shape=(jax.ShapeDtypeStruct((OWN, D), F32),...]
    pallas_call x1, Pallas kernels: 84.6 us -> 81.3 us  [body(): pl.pallas_call(kernel, out_shape=(jax.ShapeDtypeStruct((OWN, D), F32), ja...]
where the time goes in v4:
time: 84.9 us; the launch traced here: 83.5 us
  Pallas kernels  82.8 us (98%)
    pallas_call x1, Pallas kernels, body(): pl.pallas_call(kernel, out_shape=(jax.ShapeDtypeStruct((OWN, D), F32), ja...  81.3 us

profile of v4, /device:TPU:6, one launch (start us, length us, event | category | flops | bytes accessed | tf_op | source)
XLA Modules:
  0.0 83.5 jit_solution(4254771599772648852)
XLA Ops:
  0.6 81.3 %shard_map.167 = (f32[32,512]{1,0:T(8,128)}, f32[32,512]{1,0:T(8,128)}) custom-call(bf16[256,512]{1,0:T(8,128)(2,1)} %msg.1, bf16[256,512]{1,0:T(8,128)(2,1)} %dst.1, bf16[1536,512]{1,0:T(8,128)(2,1)} %nbr.1, bf16[256,512]{1,0:T(8,128)(2,1)} %emb.1, s32[1,256]{1,0:T(1,128)} %bitcast.12, s32[6,256]{1,0:T(8,128)} %bitcast.9, s32[1,256]{1,0:T(1,128)} %bitcast.13, ...), custom_call_target="tpu_custom_call" | custom-call | flops 4000000000 | bytes 8000000 | tf_op jit(solution)/shard_map/pallas_call | solution.py:532
  82.0 1.5 %shard_map.168 = (f32[32,512]{1,0:T(8,128)}, f32[32,512]{1,0:T(8,128)}) custom-call(f32[32,512]{1,0:T(8,128)} %get-tuple-element.6.ver_in, f32[32,512]{1,0:T(8,128)} %get-tuple-element.7.node_in), custom_call_target="tpu_custom_call" | custom-call | tf_op jit(solution)/shard_map/pallas_call | solution.py:551

commit v5 on v4

--- a/solution.py
+++ b/solution.py
@@ -63,11 +63,11 @@
 ):
     tm = lax.axis_index("tm")
     node = lax.axis_index("node")
-    x, y = tm // 4, tm % 4
-    z, c = node // 2, node % 2
+    x, y = tm >> 2, tm & 3
+    z, c = node >> 1, node & 1
     other = 1 - c
     sibling = (tm, z * 2 + other)
-    zq, zy = z // 4, z % 4
+    zq, zy = z >> 2, z & 3
 
     def pick(p, q):
         return jnp.where(c == 0, p, q)
@@ -77,16 +77,16 @@
     def tm_of(aa, bb):
         return pick(aa * 4 + bb, bb * 4 + aa)
 
-    a_left, a_right, a_far = (a + 3) % 4, (a + 1) % 4, (a + 2) % 4
-    b_left, b_right, b_far = (b + 3) % 4, (b + 1) % 4, (b + 2) % 4
+    a_left, a_right, a_far = (a + 3) & 3, (a + 1) & 3, (a + 2) & 3
+    b_left, b_right, b_far = (b + 3) & 3, (b + 1) & 3, (b + 2) & 3
     dev_a_left, dev_a_right = (tm_of(a_left, b), node), (tm_of(a_right, b), node)
     dev_b_left, dev_b_right = (tm_of(a, b_left), node), (tm_of(a, b_right), node)
 
     bufs = ((wa, CA), (wb, CB))
 
     def share(ph, q):
-        buf, width = bufs[ph]
-        return buf.at[q, y, c, :, pl.ds(pl.multiple_of(x * width, 128), width)]
+        buf, _ = bufs[ph]
+        return buf.at[x, q, y, c]
 
     blocks = (((w_kv, 0), (w_in, 0)), ((w_kv, CA), (w_in, CB)), ((w_out, 0), (w_hid, 0)), ((w_q, 0), (w_hid, CB)))
     for k, pair in enumerate(blocks):
@@ -100,8 +100,8 @@
     barrier = pltpu.get_barrier_semaphore()
 
     def greet(k, carry):
-        pl.semaphore_signal(barrier, inc=1, device_id=(tm, (node + 2 * k) % 32), device_id_type=MESH)
-        pl.semaphore_signal(barrier, inc=1, device_id=((tm + k) % 16, node), device_id_type=MESH)
+        pl.semaphore_signal(barrier, inc=1, device_id=(tm, (node + 2 * k) & 31), device_id_type=MESH)
+        pl.semaphore_signal(barrier, inc=1, device_id=((tm + k) & 15, node), device_id_type=MESH)
         return carry
 
     lax.fori_loop(1, 16, greet, 0)
@@ -113,11 +113,11 @@
     def _():
         for ph in range(2):
             def send(i, carry, ph=ph):
-                k = jnp.where(i % 2 == 0, 8 - i // 2, 8 + (i + 1) // 2)
+                k = jnp.where((i & 1) == 0, 8 - (i >> 1), 8 + ((i + 1) >> 1))
                 pltpu.make_async_remote_copy(
                     src_ref=share(ph, zq), dst_ref=share(ph, zq),
                     send_sem=s1_send.at[ph], recv_sem=s1_recv.at[ph, zq],
-                    device_id=(tm, ((z + k) % 16) * 2 + c), device_id_type=MESH,
+                    device_id=(tm, ((z + k) & 15) * 2 + c), device_id_type=MESH,
                 ).start()
                 return carry
             pltpu.make_async_copy(share(ph, zq), share(ph, zq), loc_sem.at[ph]).wait()
@@ -130,10 +130,10 @@
                 pltpu.make_async_copy(share(ph, q), share(ph, q), s1_recv.at[ph, q]).wait()
 
     def piece(ph, aa, bb, part=None):
-        buf, width = bufs[ph]
+        buf, _ = bufs[ph]
         xx, yy = pick(aa, bb), pick(bb, aa)
         rows = pl.ds(0, 4) if part is None else pl.ds(2 * part, 2)
-        return buf.at[rows, yy, c, :, pl.ds(pl.multiple_of(xx * width, 128), width)]
+        return buf.at[xx, rows, yy, c]
 
     def send_piece(ph, aa, bb, device, send_sem, part=None, slot=0):
         ref = piece(ph, aa, bb, part)
@@ -148,7 +148,7 @@
         pltpu.make_async_copy(ref, ref, piece_sem.at[ph, aa * 4 + bb, slot]).wait()
 
     def to_sibling(ph, bb):
-        buf, width = bufs[ph]
+        buf, _ = bufs[ph]
 
         def send(ref):
             pltpu.make_async_remote_copy(
@@ -158,11 +158,11 @@
 
         @pl.when(c == 0)
         def _():
-            send(buf.at[:, bb, 0])
+            send(buf.at[:, :, bb, 0])
 
         @pl.when(c == 1)
         def _():
-            send(buf.at[:, :, 1, :, pl.ds(pl.multiple_of(bb * width, 128), width)])
+            send(buf.at[bb, :, :, 1])
 
     def second_ring(ph, aa):
         send_piece(ph, aa, b, dev_b_left, r2_send)
@@ -204,7 +204,7 @@
         to_sibling(ph, b_far)
 
     def all_here(ph):
-        ref = bufs[ph][0].at[:, :, other]
+        ref = bufs[ph][0].at[:, :, :, other]
         pltpu.make_async_copy(ref, ref, sib_recv.at[ph]).wait()
 
     def widen(i, carry):
@@ -241,11 +241,18 @@
     step1(0)
     step2(0)
     step3(1)
+    step3(0)
     step4(1)
-    step3(0)
 
     def wide(ref, start, width):
-        return ref[:, :, :, :, pl.ds(start, width)].reshape(D, width)
+        size = ref.shape[-1]
+        out = []
+        while width:
+            block, at = divmod(start, size)
+            take = min(width, size - at)
+            out.append(ref[block, :, :, :, :, at : at + take].reshape(D, take))
+            start, width = start + take, width - take
+        return out[0] if len(out) == 1 else jnp.concatenate(out, axis=1)
 
     all_here(1)
 
@@ -353,7 +360,7 @@
         )
 
     for g, offsets in enumerate(FAR):
-        base = ((z + offsets[0]) % 16) * 64
+        base = ((z + offsets[0]) & 15) * 64
         wanted = (lax.broadcasted_iota(jnp.int32, (256, EV), 0) + base) & 1023
         hot = (wanted == src_id[...]).astype(F32).astype(BF16)
         sums = nn(hot, gmsg[...]).astype(BF16).reshape(4, 2, OWN, D)
@@ -371,7 +378,7 @@
 
     def hop(way, s):
         steps, near, last = chains[way]
-        to = (z + (last if s == len(steps) - 1 else near) + 16) % 16
+        to = (z + (last if s == len(steps) - 1 else near) + 16) & 15
         return pltpu.make_async_remote_copy(
             src_ref=nsend.at[way, s], dst_ref=nrecv.at[way, s],
             send_sem=ring_send.at[way, s], recv_sem=ring_recv.at[way, s],
@@ -421,7 +428,7 @@
             @pl.when(tm != t)
             def _(t=t):
                 pltpu.make_async_remote_copy(
-                    src_ref=vpart.at[t], dst_ref=vbuf.at[(t - tm + 15) % 16],
+                    src_ref=vpart.at[t], dst_ref=vbuf.at[(t - tm + 15) & 15],
                     send_sem=v_send, recv_sem=v_recv,
                     device_id=(t, node), device_id_type=MESH,
                 ).start()
@@ -459,19 +466,19 @@
         for s in range(len(chains[way][0])):
             hop(way, s).wait_send()
     pltpu.make_async_copy(vbuf, vbuf, v_send).wait()
-    for ph, (buf, width) in enumerate(bufs):
-        ref = buf.at[:, :, c]
+    for ph, (buf, _) in enumerate(bufs):
+        ref = buf.at[:, :, :, c]
         pltpu.make_async_copy(ref, ref, sib_send.at[ph]).wait()
-        ref = buf.at[:, 0:3, c, :, 0:width]
+        ref = buf.at[0:3, :, 0, c]
         pltpu.make_async_copy(ref, ref, r1_send.at[ph]).wait()
-        ref = buf.at[:, 0:3, c]
+        ref = buf.at[0:3, :, :, c]
         pltpu.make_async_copy(ref, ref, r2_send.at[ph]).wait()
 
     @pl.when(zy == y)
     def _():
-        ref = wa.at[:, 0, c, :, 0:1920]
+        ref = wb.at[0:3, :, 0, 0, :, 0:640]
         pltpu.make_async_copy(ref, ref, s1_send.at[0]).wait()
-        ref = wb.at[0, 0:3, :, :, 0:1920]
+        ref = wb.at[0:3, 0:3, 0, :, :, 0:640]
         pltpu.make_async_copy(ref, ref, s1_send.at[1]).wait()
 
 
@@ -488,8 +495,8 @@
     hbm = pl.BlockSpec(memory_space=pl.ANY)
     dma = pltpu.SemaphoreType.DMA
     scratch = [
-        pltpu.VMEM((4, 4, 2, 16, 2048), BF16),
-        pltpu.VMEM((4, 4, 2, 16, 3072), BF16),
+        pltpu.VMEM((4, 4, 4, 2, 16, CA), BF16),
+        pltpu.VMEM((4, 4, 4, 2, 16, CB), BF16),
         pltpu.VMEM((4, READS, 128), F32),
         pltpu.VMEM((SLOTS, EV, D), F32),
         pltpu.VMEM((READS, D), BF16),

time: 84.9 us -> 83.3 us (0.981)
  Pallas kernels: 82.8 us -> 81.3 us
    pallas_call x1, Pallas kernels: 81.3 us -> 79.8 us  [body(): pl.pallas_call(kernel, out_shape=(jax.ShapeDtypeStruct((OWN, D), F32), ja...]
where the time goes in v5:
time: 83.3 us; the launch traced here: 81.9 us
  Pallas kernels  81.3 us (98%)
    pallas_call x1, Pallas kernels, body(): pl.pallas_call(kernel, out_shape=(jax.ShapeDtypeStruct((OWN, D), F32), ja...  79.8 us

profile of v5, /device:TPU:6, one launch (start us, length us, event | category | flops | bytes accessed | tf_op | source)
XLA Modules:
  0.0 81.9 jit_solution(5454632011799446441)
XLA Ops:
  0.6 79.8 %shard_map.167 = (f32[32,512]{1,0:T(8,128)}, f32[32,512]{1,0:T(8,128)}) custom-call(bf16[256,512]{1,0:T(8,128)(2,1)} %msg.1, bf16[256,512]{1,0:T(8,128)(2,1)} %dst.1, bf16[1536,512]{1,0:T(8,128)(2,1)} %nbr.1, bf16[256,512]{1,0:T(8,128)(2,1)} %emb.1, s32[1,256]{1,0:T(1,128)} %bitcast.12, s32[6,256]{1,0:T(8,128)} %bitcast.9, s32[1,256]{1,0:T(1,128)} %bitcast.13, ...), custom_call_target="tpu_custom_call" | custom-call | flops 4000000000 | bytes 8000000 | tf_op jit(solution)/shard_map/pallas_call | solution.py:539
  80.4 1.5 %shard_map.168 = (f32[32,512]{1,0:T(8,128)}, f32[32,512]{1,0:T(8,128)}) custom-call(f32[32,512]{1,0:T(8,128)} %get-tuple-element.6.ver_in, f32[32,512]{1,0:T(8,128)} %get-tuple-element.7.node_in), custom_call_target="tpu_custom_call" | custom-call | tf_op jit(solution)/shard_map/pallas_call | solution.py:558

commit v6 on v5

--- a/solution.py
+++ b/solution.py
@@ -53,12 +53,14 @@
 
 
 def kernel(
-    msg, dst, nbr, emb, ev_time, nb_time, nb_count, src_id, dst_loc, owner, vrow,
+    msg_in, dst_in, nbr_in, emb_in, ev_in, nbt_in, cnt_in, src_in, dloc_in, own_in, vrow_in,
     w_in, w_hid, w_q, w_kv, w_out,
     ver_out, node_out,
+    msg, dst, nbr, emb, ev_time, nb_time, nb_count, src_id, dst_loc, owner, vrow,
     wa, wb, rbuf, keys, gkb, qk, gv, ctx, gates, mem, gmem, gin, gcand, gmsg, tcol, tpack, gwp, scp, wtp,
     vpart, vbuf, npart, nsib, nsend, nrecv, dpart,
-    loc_sem, s1_send, s1_recv, r1_send, r2_send, piece_sem, sib_send, sib_recv,
+    vcol, vids, idp,
+    in_sem, loc_sem, s1_send, s1_recv, r1_send, r2_send, piece_sem, sib_send, sib_recv,
     v_send, v_recv, nd_send, nd_recv, ring_send, ring_recv,
 ):
     tm = lax.axis_index("tm")
@@ -84,13 +86,23 @@
 
     bufs = ((wa, CA), (wb, CB))
 
+    kind = (y + 2 * c) & 3
+
     def share(ph, q):
         buf, _ = bufs[ph]
-        return buf.at[x, q, y, c]
+        return buf.at[x, q, kind, c]
+
+    inputs = (
+        (nbr_in, nbr), (ev_in, ev_time), (nbt_in, nb_time), (cnt_in, nb_count), (own_in, owner), (vrow_in, vrow),
+        (msg_in, msg), (dst_in, dst), (emb_in, emb), (src_in, src_id), (dloc_in, dst_loc),
+    )
+
+    def copy_in(i):
+        return pltpu.make_async_copy(inputs[i][0], inputs[i][1], in_sem.at[i])
 
     blocks = (((w_kv, 0), (w_in, 0)), ((w_kv, CA), (w_in, CB)), ((w_out, 0), (w_hid, 0)), ((w_q, 0), (w_hid, CB)))
     for k, pair in enumerate(blocks):
-        @pl.when(jnp.logical_and(zy == y, x == k))
+        @pl.when(jnp.logical_and(zy == kind, x == k))
         def _(pair=pair):
             for ph, (ref, at) in enumerate(pair):
                 pltpu.make_async_copy(
@@ -107,9 +119,11 @@
     lax.fori_loop(1, 16, greet, 0)
     pl.semaphore_signal(barrier, inc=1, device_id=sibling, device_id_type=MESH)
 
+    for i in range(11):
+        copy_in(i).start()
     pl.semaphore_wait(barrier, 31)
 
-    @pl.when(zy == y)
+    @pl.when(zy == kind)
     def _():
         for ph in range(2):
             def send(i, carry, ph=ph):
@@ -125,13 +139,13 @@
 
     def stage1_wait(ph):
         for q in range(4):
-            @pl.when(4 * q + y != z)
+            @pl.when(4 * q + kind != z)
             def _(q=q):
                 pltpu.make_async_copy(share(ph, q), share(ph, q), s1_recv.at[ph, q]).wait()
 
     def piece(ph, aa, bb, part=None):
         buf, _ = bufs[ph]
-        xx, yy = pick(aa, bb), pick(bb, aa)
+        xx, yy = pick(aa, bb), pick(bb, (aa + 2) & 3)
         rows = pl.ds(0, 4) if part is None else pl.ds(2 * part, 2)
         return buf.at[xx, rows, yy, c]
 
@@ -213,6 +227,8 @@
             rbuf[t, at, :] = nbr[at, t * 128 : (t + 1) * 128].astype(F32)
         return carry
 
+    for i in range(6):
+        copy_in(i).wait()
     lax.fori_loop(0, READS // 64, widen, 0)
     tpack[0:6, :] = (ev_time[...] - nb_time[...]).astype(F32)
     tpack[6:7, :] = nb_count[...].astype(F32)
@@ -233,6 +249,17 @@
         return carry
 
     lax.fori_loop(0, EV // 16, make_keys, 0)
+
+    for k in range(READS // 128):
+        idp[k : k + 1, :] = (owner[:, k * 128 : (k + 1) * 128] * OWN + vrow[k : k + 1, :]).astype(F32)
+    idp[12:16, :] = jnp.zeros((4, 128), F32)
+    columns = jnp.transpose(idp[...])
+    for k in range(READS // 128):
+        vcol[k * 128 : (k + 1) * 128, :] = jnp.broadcast_to(columns[:, k : k + 1], (128, 128))
+    for j in range(SLOTS):
+        vids[j : j + 1, :] = jnp.transpose(vcol[pl.ds(j, EV, stride=SLOTS), :])[0:1, :]
+    for i in range(6, 11):
+        copy_in(i).wait()
 
     step0(1)
     step0(0)
@@ -404,25 +431,18 @@
         for j in range(SLOTS):
             s0, s1 = sc[:, j : j + 1], sc[:, SLOTS + j : SLOTS + j + 1]
             w0, w1 = wt[:, j : j + 1], wt[:, SLOTS + j : SLOTS + j + 1]
-            for t in range(4):
-                cut = slice(t * 128, (t + 1) * 128)
-                rbuf[t, pl.ds(i * (16 * SLOTS) + j, 16, stride=SLOTS), :] = (
-                    (s0 * qk[0, at, cut] + s1 * qk[1, at, cut]) + (w0 * gv[0, at, cut] + w1 * gv[1, at, cut])
-                )
+            gkb[j, at, :] = (
+                (s0 * qk[0, at, :] + s1 * qk[1, at, :]) + (w0 * gv[0, at, :] + w1 * gv[1, at, :])
+            ).astype(BF16)
         return carry
 
-    def narrow(i, carry):
-        at = pl.ds(pl.multiple_of(i * 64, 64), 64)
-        for t in range(4):
-            gkb[at, t * 128 : (t + 1) * 128] = rbuf[t, at, :].astype(BF16)
-        return carry
-
     def version_sums(m):
+        wanted = (lax.broadcasted_iota(jnp.int32, (256, 128), 0) + 256 * m).astype(F32)
         ids = []
         for k in range(READS // 128):
-            vid = owner[:, k * 128 : (k + 1) * 128] * OWN + vrow[k : k + 1, :]
-            ids.append((lax.broadcasted_iota(jnp.int32, (256, 128), 0) + 256 * m == vid).astype(F32).astype(BF16))
-        sums = nn(jnp.concatenate(ids, axis=1), gkb[...]).astype(BF16)
+            vid = vids[k // 2 : k // 2 + 1, (k % 2) * 128 : (k % 2) * 128 + 128]
+            ids.append((wanted == vid).astype(F32).astype(BF16))
+        sums = nn(jnp.concatenate(ids, axis=1), gkb[...].reshape(READS, D)).astype(BF16)
         vpart[pl.ds(8 * m, 8)] = sums.reshape(8, OWN, D)
         for t in range(8 * m, 8 * m + 8):
             @pl.when(tm != t)
@@ -438,17 +458,16 @@
         part_copy(g).wait()
     chain_steps(0)
     lax.fori_loop(EV // 32, EV // 16, spread, 0)
+    version_sums(0)
     part_copy(3).wait()
     chain_steps(1)
-    lax.fori_loop(0, READS // 64, narrow, 0)
-    version_sums(0)
+    version_sums(1)
     chain_steps(2)
-    version_sums(1)
-    chain_steps(3)
 
     gdst = (nt(gin[:, 0:1024], wide(wb, 1536, 1024)) + nt(gcand[...], wide(wb, 2560, 512))) + gmem[...]
     hot = (lax.broadcasted_iota(jnp.int32, (OWN, EV), 0) == dst_loc[...]).astype(F32).astype(BF16)
     dpart[...] = mine(0) + nn(hot, gdst.astype(BF16))
+    chain_steps(3)
 
     ends = [(way, len(chains[way][0]) - 1) for way in range(4)]
     for way, s in ends:
@@ -474,7 +493,7 @@
         ref = buf.at[0:3, :, :, c]
         pltpu.make_async_copy(ref, ref, r2_send.at[ph]).wait()
 
-    @pl.when(zy == y)
+    @pl.when(zy == kind)
     def _():
         ref = wb.at[0:3, :, 0, 0, :, 0:640]
         pltpu.make_async_copy(ref, ref, s1_send.at[0]).wait()
@@ -495,11 +514,22 @@
     hbm = pl.BlockSpec(memory_space=pl.ANY)
     dma = pltpu.SemaphoreType.DMA
     scratch = [
+        pltpu.VMEM((EV, D), BF16),
+        pltpu.VMEM((EV, D), BF16),
+        pltpu.VMEM((READS, D), BF16),
+        pltpu.VMEM((EV, D), BF16),
+        pltpu.VMEM((1, EV), jnp.int32),
+        pltpu.VMEM((SLOTS, EV), jnp.int32),
+        pltpu.VMEM((1, EV), jnp.int32),
+        pltpu.VMEM((1, EV), jnp.int32),
+        pltpu.VMEM((1, EV), jnp.int32),
+        pltpu.VMEM((1, READS), jnp.int32),
+        pltpu.VMEM((READS // 128, 128), jnp.int32),
         pltpu.VMEM((4, 4, 4, 2, 16, CA), BF16),
         pltpu.VMEM((4, 4, 4, 2, 16, CB), BF16),
         pltpu.VMEM((4, READS, 128), F32),
         pltpu.VMEM((SLOTS, EV, D), F32),
-        pltpu.VMEM((READS, D), BF16),
+        pltpu.VMEM((SLOTS, EV, D), BF16),
         pltpu.VMEM((2, EV, D), F32),
         pltpu.VMEM((2, EV, D), F32),
         pltpu.VMEM((2, EV, D), BF16),
@@ -521,6 +551,10 @@
         pltpu.VMEM((4, 4, OWN, D), BF16),
         pltpu.VMEM((4, 4, OWN, D), BF16),
         pltpu.VMEM((OWN, D), F32),
+        pltpu.VMEM((READS, 128), F32),
+        pltpu.VMEM((8, EV), F32),
+        pltpu.VMEM((16, 128), F32),
+        dma((11,)),
         dma((2,)),
         dma((2,)),
         dma((2, 4)),
@@ -539,7 +573,7 @@
     version_grad, node_grad = pl.pallas_call(
         kernel,
         out_shape=(jax.ShapeDtypeStruct((OWN, D), F32), jax.ShapeDtypeStruct((OWN, D), F32)),
-        in_specs=[vmem] * 11 + [hbm] * 5,
+        in_specs=[hbm] * 16,
         out_specs=(vmem, vmem),
         scratch_shapes=scratch,
         compiler_params=pltpu.CompilerParams(

time: 83.3 us -> 80.7 us (0.969)
  Pallas kernels: 81.3 us -> 78.8 us
    pallas_call x1, Pallas kernels: 79.8 us -> 77.2 us  [body(): pl.pallas_call(kernel, out_shape=(jax.ShapeDtypeStruct((OWN, D), F32), ja...]
where the time goes in v6:
time: 80.7 us; the launch traced here: 79.4 us
  Pallas kernels  78.8 us (98%)
    pallas_call x1, Pallas kernels, body(): pl.pallas_call(kernel, out_shape=(jax.ShapeDtypeStruct((OWN, D), F32), ja...  77.2 us

profile of v6, /device:TPU:6, one launch (start us, length us, event | category | flops | bytes accessed | tf_op | source)
XLA Modules:
  0.0 79.4 jit_solution(9522499636678647569)
XLA Ops:
  0.6 77.2 %shard_map.167 = (f32[32,512]{1,0:T(8,128)}, f32[32,512]{1,0:T(8,128)}) custom-call(bf16[256,512]{1,0:T(8,128)(2,1)} %msg_in.1, bf16[256,512]{1,0:T(8,128)(2,1)} %dst_in.1, bf16[1536,512]{1,0:T(8,128)(2,1)} %nbr_in.1, bf16[256,512]{1,0:T(8,128)(2,1)} %emb_in.1, s32[1,256]{1,0:T(1,128)} %bitcast.12, s32[6,256]{1,0:T(8,128)} %bitcast.9, s32[1,256]{1,0:T(1,128)} %bitcast.13, ...), custom_call_target="tpu_custom_call" | custom-call | flops 4000000000 | bytes 8000000 | tf_op jit(solution)/shard_map/pallas_call | solution.py:573
  77.9 1.5 %shard_map.168 = (f32[32,512]{1,0:T(8,128)}, f32[32,512]{1,0:T(8,128)}) custom-call(f32[32,512]{1,0:T(8,128)} %get-tuple-element.6.ver_in, f32[32,512]{1,0:T(8,128)} %get-tuple-element.7.node_in), custom_call_target="tpu_custom_call" | custom-call | tf_op jit(solution)/shard_map/pallas_call | solution.py:592

commit v7 on v6

--- a/solution.py
+++ b/solution.py
@@ -270,6 +270,7 @@
     step3(1)
     step3(0)
     step4(1)
+    step4(0)
 
     def wide(ref, start, width):
         size = ref.shape[-1]
@@ -296,7 +297,6 @@
     gates[1] = update
     mem[...] = ((1.0 - update) * gates[2] + update * dst[...].astype(F32)).astype(BF16)
 
-    step4(0)
     all_here(0)
 
     gatt = nt(emb[...], wide(wa, 1024, 512)).astype(BF16)
@@ -444,13 +444,15 @@
             ids.append((wanted == vid).astype(F32).astype(BF16))
         sums = nn(jnp.concatenate(ids, axis=1), gkb[...].reshape(READS, D)).astype(BF16)
         vpart[pl.ds(8 * m, 8)] = sums.reshape(8, OWN, D)
-        for t in range(8 * m, 8 * m + 8):
-            @pl.when(tm != t)
-            def _(t=t):
+        for i in range(8):
+            to = 8 * m + ((tm + i) & 7)
+
+            @pl.when(to != tm)
+            def _(to=to):
                 pltpu.make_async_remote_copy(
-                    src_ref=vpart.at[t], dst_ref=vbuf.at[(t - tm + 15) & 15],
+                    src_ref=vpart.at[to], dst_ref=vbuf.at[(to - tm + 15) & 15],
                     send_sem=v_send, recv_sem=v_recv,
-                    device_id=(t, node), device_id_type=MESH,
+                    device_id=(to, node), device_id_type=MESH,
                 ).start()
 
     lax.fori_loop(0, EV // 32, spread, 0)

time: 80.7 us -> 80.1 us (level)
  Pallas kernels: 78.8 us -> 77.9 us
    pallas_call x1, Pallas kernels: 77.2 us -> 76.4 us  [body(): pl.pallas_call(kernel, out_shape=(jax.ShapeDtypeStruct((OWN, D), F32), ja...]
where the time goes in v7:
time: 80.1 us; the launch traced here: 78.6 us
  Pallas kernels  77.9 us (97%)
    pallas_call x1, Pallas kernels, body(): pl.pallas_call(kernel, out_shape=(jax.ShapeDtypeStruct((OWN, D), F32), ja...  76.4 us

profile of v7, /device:TPU:6, one launch (start us, length us, event | category | flops | bytes accessed | tf_op | source)
XLA Modules:
  0.0 78.6 jit_solution(7026165486313245615)
XLA Ops:
  0.6 76.4 %shard_map.167 = (f32[32,512]{1,0:T(8,128)}, f32[32,512]{1,0:T(8,128)}) custom-call(bf16[256,512]{1,0:T(8,128)(2,1)} %msg_in.1, bf16[256,512]{1,0:T(8,128)(2,1)} %dst_in.1, bf16[1536,512]{1,0:T(8,128)(2,1)} %nbr_in.1, bf16[256,512]{1,0:T(8,128)(2,1)} %emb_in.1, s32[1,256]{1,0:T(1,128)} %bitcast.12, s32[6,256]{1,0:T(8,128)} %bitcast.9, s32[1,256]{1,0:T(1,128)} %bitcast.13, ...), custom_call_target="tpu_custom_call" | custom-call | flops 4000000000 | bytes 8000000 | tf_op jit(solution)/shard_map/pallas_call | solution.py:575
  77.0 1.5 %shard_map.168 = (f32[32,512]{1,0:T(8,128)}, f32[32,512]{1,0:T(8,128)}) custom-call(f32[32,512]{1,0:T(8,128)} %get-tuple-element.6.ver_in, f32[32,512]{1,0:T(8,128)} %get-tuple-element.7.node_in), custom_call_target="tpu_custom_call" | custom-call | tf_op jit(solution)/shard_map/pallas_call | solution.py:594

commit v8 on v7

--- a/solution.py
+++ b/solution.py
@@ -262,15 +262,14 @@
         copy_in(i).wait()
 
     step0(1)
+    step1(1)
     step0(0)
-    step1(1)
     step2(1)
+    step3(1)
     step1(0)
     step2(0)
-    step3(1)
+    step4(1)
     step3(0)
-    step4(1)
-    step4(0)
 
     def wide(ref, start, width):
         size = ref.shape[-1]
@@ -292,6 +291,7 @@
     gi, gh = gate(2)
     gates[3] = gh
     gates[2] = jnp.tanh(gi + gates[0] * gh)
+    step4(0)
     gi, gh = gate(1)
     update = sigmoid(gi + gh)
     gates[1] = update

time: 80.1 us -> 82.9 us (1.035)
  the two profiles are of different devices: /device:TPU:6 before, /device:TPU:8 now
where the time goes in v8:
time: 82.9 us; the launch traced here: 82.8 us
  Pallas kernels  82.1 us (99%)
    pallas_call x1, Pallas kernels, body(): pl.pallas_call(kernel, out_shape=(jax.ShapeDtypeStruct((OWN, D), F32), ja...  80.6 us

profile of v8, /device:TPU:8, one launch (start us, length us, event | category | flops | bytes accessed | tf_op | source)
XLA Modules:
  0.0 82.8 jit_solution(427769553533576616)
XLA Ops:
  0.6 80.6 %shard_map.167 = (f32[32,512]{1,0:T(8,128)}, f32[32,512]{1,0:T(8,128)}) custom-call(bf16[256,512]{1,0:T(8,128)(2,1)} %msg_in.1, bf16[256,512]{1,0:T(8,128)(2,1)} %dst_in.1, bf16[1536,512]{1,0:T(8,128)(2,1)} %nbr_in.1, bf16[256,512]{1,0:T(8,128)(2,1)} %emb_in.1, s32[1,256]{1,0:T(1,128)} %bitcast.12, s32[6,256]{1,0:T(8,128)} %bitcast.9, s32[1,256]{1,0:T(1,128)} %bitcast.13, ...), custom_call_target="tpu_custom_call" | custom-call | flops 4000000000 | bytes 8000000 | tf_op jit(solution)/shard_map/pallas_call | solution.py:575
  81.3 1.5 %shard_map.168 = (f32[32,512]{1,0:T(8,128)}, f32[32,512]{1,0:T(8,128)}) custom-call(f32[32,512]{1,0:T(8,128)} %get-tuple-element.6.ver_in, f32[32,512]{1,0:T(8,128)} %get-tuple-element.7.node_in), custom_call_target="tpu_custom_call" | custom-call | tf_op jit(solution)/shard_map/pallas_call | solution.py:594

commit v9 on v7

--- a/solution.py
+++ b/solution.py
@@ -250,6 +250,12 @@
 
     lax.fori_loop(0, EV // 16, make_keys, 0)
 
+    for i in range(6, 11):
+        copy_in(i).wait()
+
+    step0(1)
+    step0(0)
+
     for k in range(READS // 128):
         idp[k : k + 1, :] = (owner[:, k * 128 : (k + 1) * 128] * OWN + vrow[k : k + 1, :]).astype(F32)
     idp[12:16, :] = jnp.zeros((4, 128), F32)
@@ -258,14 +264,10 @@
         vcol[k * 128 : (k + 1) * 128, :] = jnp.broadcast_to(columns[:, k : k + 1], (128, 128))
     for j in range(SLOTS):
         vids[j : j + 1, :] = jnp.transpose(vcol[pl.ds(j, EV, stride=SLOTS), :])[0:1, :]
-    for i in range(6, 11):
-        copy_in(i).wait()
-
-    step0(1)
-    step0(0)
+
     step1(1)
+    step1(0)
     step2(1)
-    step1(0)
     step2(0)
     step3(1)
     step3(0)

time: 80.1 us -> 78.8 us (0.984); the launches traced: 78.6 us -> 78.6 us
  no operation moved by 1% of the time
where the time goes in v9:
time: 78.8 us; the launch traced here: 78.6 us
  Pallas kernels  77.9 us (99%)
    pallas_call x1, Pallas kernels, body(): pl.pallas_call(kernel, out_shape=(jax.ShapeDtypeStruct((OWN, D), F32), ja...  76.4 us

profile of v9, /device:TPU:6, one launch (start us, length us, event | category | flops | bytes accessed | tf_op | source)
XLA Modules:
  0.0 78.6 jit_solution(497298686470185879)
XLA Ops:
  0.6 76.4 %shard_map.167 = (f32[32,512]{1,0:T(8,128)}, f32[32,512]{1,0:T(8,128)}) custom-call(bf16[256,512]{1,0:T(8,128)(2,1)} %msg_in.1, bf16[256,512]{1,0:T(8,128)(2,1)} %dst_in.1, bf16[1536,512]{1,0:T(8,128)(2,1)} %nbr_in.1, bf16[256,512]{1,0:T(8,128)(2,1)} %emb_in.1, s32[1,256]{1,0:T(1,128)} %bitcast.12, s32[6,256]{1,0:T(8,128)} %bitcast.9, s32[1,256]{1,0:T(1,128)} %bitcast.13, ...), custom_call_target="tpu_custom_call" | custom-call | flops 4000000000 | bytes 8000000 | tf_op jit(solution)/shard_map/pallas_call | solution.py:577
  77.1 1.5 %shard_map.168 = (f32[32,512]{1,0:T(8,128)}, f32[32,512]{1,0:T(8,128)}) custom-call(f32[32,512]{1,0:T(8,128)} %get-tuple-element.6.ver_in, f32[32,512]{1,0:T(8,128)} %get-tuple-element.7.node_in), custom_call_target="tpu_custom_call" | custom-call | tf_op jit(solution)/shard_map/pallas_call | solution.py:596
